TPU v7x, 256 devices: a whole 4x4x8 slice. The times are simulated.
256 devices in a mesh: tm: 16 (over x, z_lo), label: 8 (over y, z_hi), vocab: 2 (over core).
Axes of the slice: x: 4, y: 4, z: 8 (z_hi: 2, z_lo: 4; z = z_hi * 4 + z_lo), core: 2. Of those that a mesh axis runs over, the one named last changes fastest.
Arguments:
- enc_rows: bfloat16 [2, 384, 640], P(None, 'tm'), may hold values from -6 to 6
- pred_rows: bfloat16 [2, 80, 640], P(None, 'label'), may hold values from -6 to 6
- enc_weight: bfloat16 [640, 640], replicated, may hold values from -0.25 to 0.25
- pred_weight: bfloat16 [640, 640], replicated, may hold values from -0.25 to 0.25
- out_weight: bfloat16 [640, 4096], P(('tm', 'label'), 'vocab'), may hold values from -0.059814453 to 0.059814453
- teacher: bfloat16 [2, 384, 80, 4096], P(None, 'tm', 'label', 'vocab'), may hold values from 9.9658966e-05 to 1
- label_ids: int32 [2, 80], P(None, 'label'), may hold values from 0 to 4095
- frame_lengths: int32 [2], replicated, may hold values from 192 to 384, as said below
- label_lengths: int32 [2], replicated, may hold values from 40 to 80, as said below
Outputs:
- pair_loss: float32 [2, 384, 80], P(None, 'tm', 'label')
- grad_enc: float32 [2, 384, 640], P(None, 'tm')
- grad_pred: float32 [2, 80, 640], P(None, 'label')
- grad_out: float32 [640, 4096], P(('tm', 'label'), 'vocab')
Inputs may be any that keep to these rules, and one draw needn't show every extreme that they name: `frame_lengths`: the first utterance has all 384 frames, the others at least half of them. `label_lengths`: the first utterance has all 80 label positions, the others at least half of them.
All inputs are finite; a program needn't handle non-finite values.
Results may differ from a plain program's by a relative error of at most 0.0013.
Values may be sent and summed in bfloat16 or wider, within the bound.
A program may use at most 64 MiB of HBM per device.

v0:
```python
import jax
import jax.numpy as jnp
from jax import lax
from jax.sharding import PartitionSpec as P

label_weight = 0.5


def per_device(
    enc_rows,
    pred_rows,
    enc_weight,
    pred_weight,
    out_weight,
    teacher,
    label_ids,
    frame_lengths,
    label_lengths,
):
    utts, frames_dev, enc_width = enc_rows.shape
    labels_dev = pred_rows.shape[1]
    vocab_dev = teacher.shape[3]
    joint = enc_weight.shape[1]
    pairs = utts * frames_dev * labels_dev
    frame_start = lax.axis_index("tm") * frames_dev
    label_start = lax.axis_index("label") * labels_dev
    vocab_start = lax.axis_index("vocab") * vocab_dev
    enc_proj = jnp.dot(
        enc_rows.reshape(-1, enc_width), enc_weight, preferred_element_type=jnp.float32
    ).reshape(utts, frames_dev, joint)
    pred_proj = jnp.dot(
        pred_rows.reshape(-1, pred_rows.shape[2]), pred_weight, preferred_element_type=jnp.float32
    ).reshape(utts, labels_dev, joint)
    act = jnp.tanh(enc_proj[:, :, None, :] + pred_proj[:, None, :, :]).reshape(pairs, joint)
    hidden = act.astype(jnp.bfloat16)
    forward_weight = lax.all_gather(out_weight, ("tm", "label"), axis=0, tiled=True)
    logits = jnp.dot(hidden, forward_weight, preferred_element_type=jnp.float32)
    frame_pos = frame_start + jnp.arange(frames_dev, dtype=jnp.int32)
    label_pos = label_start + jnp.arange(labels_dev, dtype=jnp.int32)
    frame_ok = (frame_pos[None, :] < frame_lengths[:, None]).astype(jnp.float32)
    label_ok = (label_pos[None, :] < label_lengths[:, None]).astype(jnp.float32)
    mask = (frame_ok[:, :, None] * label_ok[:, None, :]).reshape(pairs)
    local_ids = jnp.broadcast_to(
        (label_ids - vocab_start)[:, None, :], (utts, frames_dev, labels_dev)
    ).reshape(pairs)
    hot = (local_ids[:, None] == jnp.arange(vocab_dev, dtype=jnp.int32)[None, :]).astype(
        jnp.float32
    )
    post = teacher.reshape(pairs, vocab_dev).astype(jnp.float32)
    expsum, total, entropy, cross, picked = lax.psum(
        (
            jnp.sum(jnp.exp(logits), axis=1),
            jnp.sum(post, axis=1),
            jnp.sum(post * jnp.log(post), axis=1),
            jnp.sum(post * logits, axis=1),
            jnp.sum(hot * logits, axis=1),
        ),
        "vocab",
    )
    lse = jnp.log(expsum)
    loss = mask * (
        entropy / total - jnp.log(total) - cross / total + lse + label_weight * (lse - picked)
    )
    student = jnp.exp(logits - lse[:, None])
    dlog = (
        mask[:, None] * (student - post / total[:, None] + label_weight * (student - hot))
    ).astype(jnp.bfloat16)
    backward_weight = lax.all_gather(out_weight, ("tm", "label"), axis=0, tiled=True)
    back = lax.dot_general(
        dlog, backward_weight, (((1,), (1,)), ((), ())), preferred_element_type=jnp.float32
    )
    slope = back * (1.0 - act * act)
    slope = slope.reshape(utts, frames_dev, labels_dev, joint)
    enc_sum = lax.psum(jnp.sum(slope, axis=2), ("label", "vocab"))
    pred_sum = lax.psum(jnp.sum(slope, axis=1), ("tm", "vocab"))
    grad_enc = jnp.dot(
        enc_sum.reshape(-1, joint),
        enc_weight.astype(jnp.float32).T,
        precision=lax.Precision.HIGHEST,
    ).reshape(utts, frames_dev, enc_width)
    grad_pred = jnp.dot(
        pred_sum.reshape(-1, joint),
        pred_weight.astype(jnp.float32).T,
        precision=lax.Precision.HIGHEST,
    ).reshape(utts, labels_dev, pred_weight.shape[0])
    weight_term = lax.dot_general(
        hidden, dlog, (((0,), (0,)), ((), ())), preferred_element_type=jnp.float32
    )
    grad_out = lax.psum_scatter(weight_term, ("tm", "label"), scatter_dimension=0, tiled=True)
    return (loss.reshape(utts, frames_dev, labels_dev), grad_enc, grad_pred, grad_out)


def solution(mesh):
    return jax.shard_map(
        per_device,
        mesh=mesh,
        in_specs=(
            P(None, "tm", None),
            P(None, "label", None),
            P(),
            P(),
            P(("tm", "label"), "vocab"),
            P(None, "tm", "label", "vocab"),
            P(None, "label"),
            P(),
            P(),
        ),
        out_specs=(
            P(None, "tm", "label"),
            P(None, "tm", None),
            P(None, "label", None),
            P(("tm", "label"), "vocab"),
        ),
        check_vma=False,
    )
```

profile of v0, /device:TPU:1, one launch (start us, length us, event | category | flops | bytes accessed | tf_op | source)
XLA Modules:
  0.0 1134.6 jit_solution(1702195514717276132)
XLA Ops:
  7.2 0.0 copy-start
  7.2 0.0 all-gather.3.cloned.1.call-start
  7.2 0.7 all-gather.3.cloned.1.call-update
  7.9 0.0 all-reduce.5.cloned.1.call-start
  8.0 0.7 broadcast_subtract_fusion
  8.7 0.1 eq.15
  8.8 5.6 copy.22
  14.4 0.0 copy-start.1
  14.4 0.0 copy-start.5
  14.4 0.0 copy-start.6
  14.4 5.3 reshape.135
  19.8 0.0 copy-done.1
  19.8 0.0 copy-done.5
  19.8 0.2 fusion.4
  20.0 0.0 copy-done
  20.0 0.0 copy-done.6
  20.1 0.0 copy-start.7
  20.1 0.0 copy-start.8
  20.1 0.3 fusion.8
  20.3 1.3 multiply_subtract_fusion
  21.7 1.4 convert_element_type.44
  23.0 2.5 fusion
  25.5 0.1 copy.21
  25.6 0.1 reduce_sum.70
  25.7 0.1 copy.20
  25.8 0.1 reduce_sum.68
  26.0 0.0 copy-done.7
  26.0 0.1 compare_convert_fusion
  26.1 0.0 copy-done.8
  26.1 0.1 compare_convert_fusion.1
  26.1 0.1 broadcast_multiply_fusion
  26.2 0.1 mul.75
  26.3 1.3 sub.49
  27.6 574.3 %all-gather.3.cloned.1.call-done = bf16[128,5,2048]{2,1,0:T(8,128)(2,1)} async-done(((bf16[1,5,2048]{2,1,0:T(8,128)(2,1)}), bf16[128,5,2048]{2,1,0:T(8,128)(2,1)}) %all-gather.3.cloned.1.call-update) | async-done | bytes 2621456 | tf_op jit(solution)/shard_map/all_gather | solution.py:36
  601.9 5.6 reshape.137
  607.5 6.9 exponential_reduce_fusion
  614.4 89.5 %all-reduce.1 = (f32[480]{0:T(512)S(1)}, f32[480]{0:T(512)S(1)}, f32[480]{0:T(512)S(1)}, f32[480]{0:T(512)S(1)}, f32[480]{0:T(512)S(1)}) all-reduce(f32[480]{0:T(512)S(1)} %get-tuple-element.17, f32[480]{0:T(512)S(1)} %get-tuple-element.18, f32[480]{0:T(512)S(1)} %reduce_sum.70, ...), channel_id=1, replica_groups=mesh['tm'=16,'label'=8,'vocab'=2] {'vocab'}, use_global_device_ids=true, to_apply=%region_9.0 | all-reduce | flops 2400 | bytes 19200 | tf_op jit(solution)/shard_map/psum | solution.py:50
  704.0 0.0 copy-start.3
  704.0 0.0 copy-start.4
  704.0 4.5 multiply_convert_fusion
  708.5 0.0 copy-done.3
  708.5 0.0 copy-done.4
  708.5 2.8 convolution_multiply_fusion
  711.3 2.6 reshape.134
  713.8 2.6 fusion.11
  716.4 0.0 all-reduce.5.cloned.1.call-update
  716.4 0.0 all-reduce.7.cloned.1.call-start
  716.5 3.9 fusion.13
  720.4 0.0 copy-start.9
  720.4 0.0 copy-start.2
  720.4 0.0 all-reduce.7.cloned.1.call-update
  720.4 0.6 copy-done.9
  721.1 0.6 dynamic-slice
  722.3 0.1 reshape.133
  722.4 0.7 copy.24
  723.1 132.8 %psum.55 = f32[2,10,640]{2,1,0:T(8,128)S(1)} all-reduce(f32[2,10,640]{2,1,0:T(8,128)S(1)} %get-tuple-element.19), channel_id=1, replica_groups=mesh['tm'=16,'label'=8,'vocab'=2] {'tm','vocab'}, use_global_device_ids=true, to_apply=%region_13.0 | all-reduce | flops 12800 | bytes 102400 | tf_op jit(solution)/shard_map/psum | solution.py:75
  855.9 0.0 copy-done.2
  855.9 0.8 fusion.2
  856.7 0.7 copy.25
  857.4 26.9 %all-reduce.5.cloned.1.call-done = f32[2,24,640]{2,1,0:T(8,128)} async-done(((f32[2,24,640]{2,1,0:T(8,128)}), f32[2,24,640]{2,1,0:T(8,128)}) %all-reduce.5.cloned.1.call-update) | async-done | bytes 122896 | tf_op jit(solution)/shard_map/psum | solution.py:74
  884.3 2.4 fusion.6
  886.7 239.8 %all-reduce.7.cloned.1.call-done = f32[640,2048]{1,0:T(8,128)} async-done(((f32[640,2048]{1,0:T(8,128)}), f32[640,2048]{1,0:T(8,128)}) %all-reduce.7.cloned.1.call-update) | async-done | bytes 5242896
  1126.5 1.5 constant_dynamic-slice_fusion
  (4 shorter events, 0.0 us)
Async XLA Ops:
  7.2 12.9 %copy-start = (bf16[640,640]{1,0:T(8,128)(2,1)S(1)}, bf16[640,640]{1,0:T(8,128)(2,1)}, u32[]{:S(2)}) copy-start(bf16[640,640]{1,0:T(8,128)(2,1)} %param.11) | copy-start | bytes 2457604
  7.2 594.7 %all-gather.3.cloned.1.call-start = ((), (), s32[]{:S(2)}) async-start(), calls=%async_computation.1 | async-start | bytes 4227072 | tf_op jit(solution)/shard_map/all_gather | solution.py:36
  7.9 876.4 %all-reduce.5.cloned.1.call-start = ((), (), s32[]{:S(2)}) async-start(), calls=%async_computation | async-start | bytes 245760 | tf_op jit(solution)/shard_map/psum | solution.py:74
  14.4 5.4 copy-start.1
  14.4 5.4 copy-start.5
  14.4 5.6 copy-start.6
  20.1 5.9 copy-start.7
  20.1 6.0 copy-start.8
  704.0 4.5 copy-start.3
  704.0 4.5 copy-start.4
  716.4 410.1 %all-reduce.7.cloned.1.call-start = ((), (), s32[]{:S(2)}) async-start(), calls=%async_computation.2 | async-start | bytes 10485760
  720.4 0.7 copy-start.9
  720.4 135.5 %copy-start.2 = (bf16[640,640]{1,0:T(8,128)(2,1)S(1)}, bf16[640,640]{1,0:T(8,128)(2,1)}, u32[]{:S(2)}) copy-start(bf16[640,640]{1,0:T(8,128)(2,1)} %param.12) | copy-start | bytes 2457604
Sparse Core Ops, SparseCore 0:
  9.8 592.0 all-gather.2
  716.6 167.6 all-reduce.4
  890.7 235.8 all-reduce.6
where the time goes:
time: 1140 us; the launch traced here: 1130 us
  waiting for transfers between devices  842 us (74%)
  blocking collectives  222 us (19%)
  local copies, waits for them, and re-layouts  26.7 us (2%)
  matrix products  17.4 us (2%)
  between operations  14.6 us (1%)
  other arithmetic  11.8 us (1%)
    all_gather x1, waiting for transfers between devices, per_device(): lax.all_gather(out_weight, ('tm', 'label'), axis=0, tiled=True)  574 us
    unnamed x4, waiting for transfers between devices  241 us
    psum x1, blocking collectives, per_device(): pred_sum = lax.psum(jnp.sum(slope, axis=1), ('tm', 'vocab'))  133 us
    psum x1, blocking collectives, per_device(): lax.psum((jnp.sum(jnp.exp(logits), axis=1), jnp.sum(post, axis=1), jnp.su...  89.5 us
    psum x1, waiting for transfers between devices, per_device(): enc_sum = lax.psum(jnp.sum(slope, axis=2), ('label', 'vocab'))  26.9 us
  transfers between devices with their start and end apart: 3, of which 3 were waited for; matrix products, arithmetic and copies ran while one was open for 3% of the time, Pallas kernels for 0%

commit v1 on v0

v1 whole, which is shorter than its diff:
```python
import functools

import jax
import jax.numpy as jnp
from jax import lax
from jax.experimental import pallas as pl
from jax.experimental.pallas import tpu as pltpu
from jax.sharding import PartitionSpec as P

MESH = pl.DeviceIdType.MESH
F32, BF16 = jnp.float32, jnp.bfloat16
label_weight = 0.5

SIZE = {"x": 4, "y": 4, "z": 8}
ORDERS = (("z", "y", "x"), ("z", "x", "y"), ("z", "y", "x"), ("z", "x", "y"), ("y", "x", "z"))
CHUNKS = len(ORDERS)
BLOCKS = 128
UTTS, FRAMES, LABELS = 2, 24, 10
ROWS = UTTS * FRAMES
PAIRS = ROWS * LABELS
PADDED = 512
JOINT = 640
VOCAB = 2048
TILES = VOCAB // 128
MAIN = ROWS * 8
SIDE = 40


def nt(a, b):
    return lax.dot_general(a, b, (((1,), (1,)), ((), ())), preferred_element_type=F32)


def nn(a, b):
    return jnp.dot(a, b, preferred_element_type=F32)


def split3(value):
    first = value.astype(BF16)
    rest = value - first.astype(F32)
    second = rest.astype(BF16)
    third = (rest - second.astype(F32)).astype(BF16)
    return first, second, third


def pair_place(p):
    tail = p - MAIN
    frame = jnp.where(p < MAIN, p >> 3, tail >> 1)
    label = jnp.where(p < MAIN, p & 7, 8 + (tail & 1))
    return frame, label, (frame >= FRAMES).astype(jnp.int32)


def kernel(
    frame_len, label_len, ids, enc_rows, pred_rows, own_weight, enc_weight_hbm, pred_weight_hbm, teacher_hbm,
    loss_out, enc_out, pred_out, grad_out,
    raw, weight, wide, hidden, hidden_t, act, post, expo, dlog, teacher, enc_weight, pred_weight, perm,
    proj, stats, stats_in, ident, mask, scale_a, scale_b, acc, term, ring_in, mid_in, last_in,
    side, side_in, pair_in, y_in, x_in, zh_in, zl_in, side_nat, grads, grads_in, result,
    local_sem, send_sem, recv_sem,
):
    tm, lab, core = lax.axis_index("tm"), lax.axis_index("label"), lax.axis_index("vocab")
    at = {"x": tm // 4, "y": lab // 2, "z": (lab % 2) * 4 + tm % 4}

    def device(axis, coordinate):
        where = dict(at)
        where[axis] = coordinate
        return (where["x"] * 4 + where["z"] % 4, where["y"] * 2 + where["z"] // 4, core)

    def around(axis, distance):
        return lax.rem(at[axis] + distance + SIZE[axis], SIZE[axis])

    sent = []

    def send(src, dst, target):
        number = len(sent)
        copy = pltpu.make_async_remote_copy(
            src_ref=src, dst_ref=dst, send_sem=send_sem.at[number], recv_sem=recv_sem.at[number],
            device_id=target, device_id_type=MESH,
        )
        copy.start()
        sent.append(copy)
        return copy

    local = []
    for number, (src, dst) in enumerate(((enc_weight_hbm, enc_weight), (pred_weight_hbm, pred_weight), (teacher_hbm, teacher))):
        copy = pltpu.make_async_copy(src, dst, local_sem.at[number])
        copy.start()
        local.append(copy)

    barrier = pltpu.get_barrier_semaphore()
    partners = [device(a, around(a, d)) for a in "xyz" for d in range(1, SIZE[a])] + [(tm, lab, 1 - core)]
    for target in partners:
        pl.semaphore_signal(barrier, inc=1, device_id=target, device_id_type=MESH)

    own = own_weight[...].astype(F32)
    for r in range(CHUNKS):
        for c in range(TILES):
            result[r, c : c + 1, :] = own[r : r + 1, c * 128 : (c + 1) * 128]

    def spot(r):
        first, middle, last = ORDERS[r]
        return (at[last] * SIZE[middle] + at[middle]) * SIZE[first] + at[first]

    for r in range(CHUNKS):
        raw[r, pl.ds(pl.multiple_of(spot(r) * 16, 16), 16), :] = result[r].astype(BF16)

    pl.semaphore_wait(barrier, len(partners))

    first_copies = []
    for r in range(CHUNKS):
        axis = ORDERS[r][0]
        block = raw.at[r, pl.ds(pl.multiple_of(spot(r) * 16, 16), 16), :]
        first_copies.append([send(block, block, device(axis, around(axis, d))) for d in range(1, SIZE[axis])])

    p = lax.broadcasted_iota(jnp.int32, (PADDED, 128), 0)
    lane = lax.broadcasted_iota(jnp.int32, (PADDED, 128), 1)
    frame, label, utt = pair_place(p)
    frame_ok = tm * FRAMES + frame - FRAMES * utt < jnp.where(utt == 1, frame_len[1], frame_len[0])
    label_ok = lab * LABELS + label < jnp.where(utt == 1, label_len[1], label_len[0])
    mask[...] = jnp.where(frame_ok & label_ok, 1.0, 0.0)[:PAIRS]
    emitted = jnp.zeros((PADDED, 128), jnp.int32)
    for k in range(LABELS):
        emitted = jnp.where(label == k, jnp.where(utt == 1, ids[1, k], ids[0, k]), emitted)
    ident[...] = (emitted - core * VOCAB)[:PAIRS]
    spread = jnp.where((lane == frame) | (lane == ROWS + 16 * utt + label), 1.0, 0.0).astype(BF16)

    j = lax.broadcasted_iota(jnp.int32, (JOINT, BLOCKS), 0)
    block_at = lax.broadcasted_iota(jnp.int32, (JOINT, BLOCKS), 1)
    for r in range(CHUNKS):
        first, middle, last = ORDERS[r]
        n1, n2 = SIZE[first], SIZE[middle]
        coords = {first: block_at % n1, middle: (block_at // n1) % n2, last: block_at // (n1 * n2)}
        natural = coords["x"] * 32 + (coords["z"] % 4) * 8 + coords["y"] * 2 + coords["z"] // 4
        perm[:, r * BLOCKS : (r + 1) * BLOCKS] = jnp.where(j == natural * CHUNKS + r, 1.0, 0.0).astype(BF16)

    second_copies = []
    for r in range(CHUNKS):
        first, middle, last = ORDERS[r]
        for copy in first_copies[r]:
            copy.wait_recv()
        rows = SIZE[first] * 16
        block = raw.at[r, pl.ds(pl.multiple_of((at[last] * SIZE[middle] + at[middle]) * rows, 16), rows), :]
        second_copies.append([send(block, block, device(middle, around(middle, d))) for d in range(1, SIZE[middle])])

    local[0].wait()
    local[1].wait()
    proj[...] = jnp.zeros_like(proj)
    for b in range(UTTS):
        proj[b * FRAMES : (b + 1) * FRAMES, :] = enc_rows[b].astype(F32)
        proj[ROWS + 16 * b : ROWS + 16 * b + LABELS, :] = pred_rows[b].astype(F32)
    proj[0:ROWS, :] = nn(proj[0:ROWS, :].astype(BF16), enc_weight[...])
    proj[ROWS : ROWS + 32, :] = nn(proj[ROWS : ROWS + 32, :].astype(BF16), pred_weight[...])
    ordered = sum(nn(part, perm[...]) for part in split3(proj[...]))
    proj[...] = ordered

    def block_of(ref, r, coordinate, half=None):
        first, middle, last = ORDERS[r]
        rows = SIZE[first] * SIZE[middle] * 16
        start = coordinate * rows
        if half is not None:
            rows //= 2
            start = start + half * rows
        return ref.at[r, pl.ds(pl.multiple_of(start, 16), rows), :]

    def ring_gather(r, step):
        axis = ORDERS[r][2]
        n = SIZE[axis]
        copies = []
        for way, half in ((1, 0), (-1, 1)):
            block = block_of(raw, r, around(axis, -way * step), half if step == n // 2 - 1 else None)
            copies.append(send(block, block, device(axis, around(axis, way))))
        return copies

    ring = {}
    for r in range(CHUNKS):
        for copy in second_copies[r]:
            copy.wait_recv()
        ring[r, 0] = ring_gather(r, 0)

    act[...] = jnp.tanh(sum(nn(spread, part) for part in split3(proj[...])))
    hidden[...] = act[...].astype(BF16)
    hidden_t[...] = act[...].T.astype(BF16)

    def ring_next(r, step):
        for copy in ring[r, step - 1]:
            copy.wait_recv()
        ring[r, step] = ring_gather(r, step)

    for r in range(CHUNKS):
        ring_next(r, 1)

    local[2].wait()
    lane8 = lax.broadcasted_iota(jnp.int32, (8, 128), 1)

    def teacher_rows(rows, start):
        post[pl.ds(pl.multiple_of(start, 8), 8), :] = rows
        total = jnp.sum(rows, axis=1, keepdims=True)
        ent = jnp.sum(rows * jnp.log(rows), axis=1, keepdims=True)
        stats[pl.ds(pl.multiple_of(start, 8), 8), :] = jnp.where(lane8 == 1, total, jnp.where(lane8 == 2, ent, 0.0))

    def teacher_step(g, carry):
        tails = []
        for k in range(4):
            rows = teacher[4 * g + k].astype(F32)
            teacher_rows(rows[0:8], 32 * g + 8 * k)
            tails.append(rows[8:10])
        teacher_rows(jnp.concatenate(tails, axis=0), MAIN + 8 * g)
        return carry

    lax.fori_loop(0, 4, teacher_step, 0)
    ring_next(4, 2)
    lax.fori_loop(4, 8, teacher_step, 0)
    ring_next(4, 3)
    lax.fori_loop(8, 12, teacher_step, 0)

    for r in range(CHUNKS):
        for copy in ring[r, SIZE[ORDERS[r][2]] // 2 - 1]:
            copy.wait_recv()
        wide[...] = raw[r].astype(F32)
        for c in range(TILES):
            weight[r * BLOCKS : (r + 1) * BLOCKS, c * 128 : (c + 1) * 128] = wide[pl.ds(c, BLOCKS, stride=16), :].astype(BF16)

    acc[...] = jnp.zeros_like(acc)
    lanes = lax.broadcasted_iota(jnp.int32, (PAIRS, 128), 1)
    width = 512
    for start in range(0, VOCAB, width):
        logits = nn(hidden[0:PAIRS, :], weight[:, start : start + width])
        powers = jnp.exp(logits)
        expo[:, start : start + width] = powers
        for c in range(0, width, 128):
            part = logits[:, c : c + 128]
            acc[0] += powers[:, c : c + 128]
            acc[1] += post[:, start + c : start + c + 128] * part
            acc[2] += jnp.where(lanes + (start + c) == ident[...], part, 0.0)
    expsum = jnp.sum(acc[0], axis=1, keepdims=True)
    cross = jnp.sum(acc[1], axis=1, keepdims=True)
    picked = jnp.sum(acc[2], axis=1, keepdims=True)
    stats[...] += jnp.where(lanes == 0, expsum, jnp.where(lanes == 3, cross, jnp.where(lanes == 4, picked, 0.0)))
    other_core = (tm, lab, 1 - core)
    stats_copy = send(stats, stats_in, other_core)
    dlog[PAIRS:PADDED, :] = jnp.zeros((PADDED - PAIRS, VOCAB), BF16)
    stats_copy.wait_recv()

    sums = stats[...] + stats_in[...]
    expsum, total, ent, cross, picked = (sums[:, k : k + 1] for k in range(5))
    scale_a[...] = (1.0 + label_weight) * mask[...] / expsum
    scale_b[...] = mask[...] / total
    lse = jnp.log(expsum)
    pair_loss = ent / total - jnp.log(total) - cross / total + lse + label_weight * (lse - picked)

    def dlog_step(g, carry):
        rows = pl.ds(pl.multiple_of(32 * g, 32), 32)
        a, b, hot, ident_g = scale_a[rows, :], scale_b[rows, :], label_weight * mask[rows, :], ident[rows, :]
        lane_g = lax.broadcasted_iota(jnp.int32, (32, 128), 1)
        for c in range(TILES):
            columns = slice(c * 128, (c + 1) * 128)
            value = a * expo[rows, columns] - b * post[rows, columns]
            dlog[rows, columns] = (value - jnp.where(lane_g + c * 128 == ident_g, hot, 0.0)).astype(BF16)
        return carry

    lax.fori_loop(0, PAIRS // 32, dlog_step, 0)

    def term_block(r, coordinate, half=None):
        return block_of(term, r, coordinate, half)

    def ring_reduce(r, step):
        axis = ORDERS[r][2]
        n = SIZE[axis]
        rows = BLOCKS * 16 // n
        copies = []
        for way, half, slot in ((1, 0, 0), (-1, 1, 1)):
            distance = n // 2 - step
            block = term_block(r, around(axis, way * distance), half if step == 0 else None)
            size = rows // 2 if step == 0 else rows
            place = ring_in.at[r, pl.ds((2 * step + slot) * rows, size), :]
            copies.append(send(block, place, device(axis, around(axis, way))))
        return copies

    def ring_add(r, step):
        axis = ORDERS[r][2]
        n = SIZE[axis]
        rows = BLOCKS * 16 // n
        for copy in ring[r, step]:
            copy.wait_recv()
        for way, half, slot in ((1, 0, 0), (-1, 1, 1)):
            distance = n // 2 - step - 1
            size = rows // 2 if step == 0 else rows
            start = around(axis, way * distance) * rows + (half * size if step == 0 else 0)
            place = pl.ds(pl.multiple_of(start, 16), size)
            base = (2 * step + slot) * rows
            term[r, place, :] += ring_in[r, base : base + size, :]

    for r in range(CHUNKS):
        product = nn(hidden_t[r * BLOCKS : (r + 1) * BLOCKS, :], dlog[...])
        for c in range(TILES):
            term[r, pl.ds(c, BLOCKS, stride=16), :] = product[:, c * 128 : (c + 1) * 128]
        ring[r, 0] = ring_reduce(r, 0)

    back = nt(dlog[...], weight[...])
    slope = back * (1.0 - act[...] * act[...])
    q = lax.broadcasted_iota(jnp.int32, (2 * SIDE, PADDED), 0)
    frame_p, label_p, utt_p = pair_place(lax.broadcasted_iota(jnp.int32, (2 * SIDE, PADDED), 1))
    utt_q = (q >= SIDE).astype(jnp.int32)
    place_q = q - SIDE * utt_q
    is_enc = (place_q < FRAMES) & (frame_p == FRAMES * utt_q + place_q)
    is_pred = (place_q >= FRAMES) & (utt_p == utt_q) & (label_p == place_q - FRAMES)
    gather_sums = jnp.where(is_enc | is_pred, 1.0, 0.0).astype(BF16)
    side[...] = sum(nn(gather_sums, part) for part in split3(slope))
    theirs = side.at[pl.ds(pl.multiple_of((1 - core) * SIDE, 8), SIDE), :]
    pair_copy = send(theirs, pair_in, other_core)

    for r in range(CHUNKS):
        ring_add(r, 0)
        ring[r, 1] = ring_reduce(r, 1)

    pair_copy.wait_recv()
    side_nat[...] = side[pl.ds(pl.multiple_of(core * SIDE, 8), SIDE), :] + pair_in[...]
    enc_part, pred_part = side_nat.at[0:FRAMES, :], side_nat.at[FRAMES:SIDE, :]
    y_copies = [send(enc_part, y_in.at[d - 1], device("y", around("y", d))) for d in range(1, 4)]
    x_copies = [send(pred_part, x_in.at[d - 1], device("x", around("x", d))) for d in range(1, 4)]

    _, label_c, _ = pair_place(lax.broadcasted_iota(jnp.int32, (PAIRS, 128), 0))
    acc[0] = jnp.where(lanes == label_c, mask[...] * pair_loss, 0.0)
    losses = jnp.concatenate([acc[0], jnp.zeros((PADDED - PAIRS, 128), F32)], axis=0)
    table = sum(nn(gather_sums, part) for part in split3(losses))
    for b in range(UTTS):
        loss_out[b] = table[SIDE * b : SIDE * b + FRAMES, 0:LABELS]

    ring_add(4, 1)
    ring[4, 2] = ring_reduce(4, 2)

    for copy in y_copies + x_copies:
        copy.wait_recv()
    side_in[0:FRAMES, :] = side_nat[0:FRAMES, :] + y_in[0] + y_in[1] + y_in[2]
    side_in[FRAMES:SIDE, :] = side_nat[FRAMES:SIDE, :] + x_in[0] + x_in[1] + x_in[2]
    z_low, z_high = at["z"] % 4, at["z"] // 4
    zh_copy = send(side_in.at[0:FRAMES, :], zh_in, device("z", around("z", 4)))
    zl_copies = [
        send(side_in.at[FRAMES:SIDE, :], zl_in.at[d - 1], device("z", z_high * 4 + (z_low + d) % 4)) for d in range(1, 4)
    ]

    ring_add(4, 2)
    ring[4, 3] = ring_reduce(4, 3)

    mid_copies = {}

    def finish_ring(r):
        first, middle, last = ORDERS[r]
        ring_add(r, SIZE[last] // 2 - 1)
        rows = SIZE[first] * 16
        mid_copies[r] = []
        for d in range(1, SIZE[middle]):
            start = (at[last] * SIZE[middle] + around(middle, d)) * rows
            block = term.at[r, pl.ds(pl.multiple_of(start, 16), rows), :]
            mid_copies[r].append(send(block, mid_in.at[r, d - 1, 0:rows, :], device(middle, around(middle, d))))

    last_copies = {}

    def finish_mid(r):
        first, middle, last = ORDERS[r]
        rows = SIZE[first] * 16
        for copy in mid_copies[r]:
            copy.wait_recv()
        start = (at[last] * SIZE[middle] + at[middle]) * rows
        place = pl.ds(pl.multiple_of(start, 16), rows)
        term[r, place, :] = term[r, place, :] + mid_in[r, 0, 0:rows, :] + mid_in[r, 1, 0:rows, :] + mid_in[r, 2, 0:rows, :]
        last_copies[r] = []
        for d in range(1, SIZE[first]):
            block = term.at[r, pl.ds(pl.multiple_of(start + around(first, d) * 16, 16), 16), :]
            last_copies[r].append(send(block, last_in.at[r, d - 1], device(first, around(first, d))))

    for r in range(CHUNKS):
        finish_ring(r)

    zh_copy.wait_recv()
    for copy in zl_copies:
        copy.wait_recv()
    side_nat_value = jnp.concatenate(
        [side_in[0:FRAMES, :] + zh_in[...], side_in[FRAMES:SIDE, :] + zl_in[0] + zl_in[1] + zl_in[2]], axis=0
    )
    natural = sum(nt(part, perm[...]) for part in split3(side_nat_value))
    grads[0:FRAMES, :] = sum(nt(part, enc_weight[...]) for part in split3(natural[0:FRAMES]))
    grads[FRAMES:SIDE, :] = sum(nt(part, pred_weight[...]) for part in split3(natural[FRAMES:SIDE]))
    grads_copy = send(grads, grads_in, other_core)

    for r in range(CHUNKS):
        finish_mid(r)

    enc_out[core] = grads[0:FRAMES, :]
    pred_out[core] = grads[FRAMES : FRAMES + LABELS, :]
    grads_copy.wait_recv()
    enc_out[1 - core] = grads_in[0:FRAMES, :]
    pred_out[1 - core] = grads_in[FRAMES : FRAMES + LABELS, :]

    for r in range(CHUNKS):
        for copy in last_copies[r]:
            copy.wait_recv()
        total_r = term[r, pl.ds(pl.multiple_of(spot(r) * 16, 16), 16), :]
        for d in range(1, SIZE[ORDERS[r][0]]):
            total_r = total_r + last_in[r, d - 1]
        result[r] = total_r
        for c in range(TILES):
            grad_out[r : r + 1, c * 128 : (c + 1) * 128] = result[r, c : c + 1, :]

    for copy in sent:
        copy.wait_send()


def per_device(
    enc_rows, pred_rows, enc_weight, pred_weight, out_weight, teacher, label_ids, frame_lengths, label_lengths
):
    vmem, smem, anywhere = (pl.BlockSpec(memory_space=s) for s in (pltpu.VMEM, pltpu.SMEM, pl.ANY))
    scratch = [
        pltpu.VMEM((CHUNKS, BLOCKS * 16, 128), BF16),
        pltpu.VMEM((JOINT, VOCAB), BF16),
        pltpu.VMEM((BLOCKS * 16, 128), F32),
        pltpu.VMEM((PADDED, JOINT), BF16),
        pltpu.VMEM((JOINT, PADDED), BF16),
        pltpu.VMEM((PADDED, JOINT), F32),
        pltpu.VMEM((PAIRS, VOCAB), F32),
        pltpu.VMEM((PAIRS, VOCAB), F32),
        pltpu.VMEM((PADDED, VOCAB), BF16),
        pltpu.VMEM((ROWS, LABELS, VOCAB), BF16),
        pltpu.VMEM((JOINT, JOINT), BF16),
        pltpu.VMEM((JOINT, JOINT), BF16),
        pltpu.VMEM((JOINT, JOINT), BF16),
        pltpu.VMEM((128, JOINT), F32),
        pltpu.VMEM((PAIRS, 128), F32),
        pltpu.VMEM((PAIRS, 128), F32),
        pltpu.VMEM((PAIRS, 128), jnp.int32),
        pltpu.VMEM((PAIRS, 128), F32),
        pltpu.VMEM((PAIRS, 128), F32),
        pltpu.VMEM((PAIRS, 128), F32),
        pltpu.VMEM((3, PAIRS, 128), F32),
        pltpu.VMEM((CHUNKS, BLOCKS * 16, 128), F32),
        pltpu.VMEM((CHUNKS, BLOCKS * 16, 128), F32),
        pltpu.VMEM((CHUNKS, 3, 128, 128), F32),
        pltpu.VMEM((CHUNKS, 7, 16, 128), F32),
        pltpu.VMEM((2 * SIDE, JOINT), F32),
        pltpu.VMEM((SIDE, JOINT), F32),
        pltpu.VMEM((SIDE, JOINT), F32),
        pltpu.VMEM((3, FRAMES, JOINT), F32),
        pltpu.VMEM((3, SIDE - FRAMES, JOINT), F32),
        pltpu.VMEM((FRAMES, JOINT), F32),
        pltpu.VMEM((3, SIDE - FRAMES, JOINT), F32),
        pltpu.VMEM((SIDE, JOINT), F32),
        pltpu.VMEM((SIDE, JOINT), F32),
        pltpu.VMEM((SIDE, JOINT), F32),
        pltpu.VMEM((CHUNKS, 16, 128), F32),
        pltpu.SemaphoreType.DMA((3,)),
        pltpu.SemaphoreType.DMA((160,)),
        pltpu.SemaphoreType.DMA((160,)),
    ]
    return pl.pallas_call(
        kernel,
        out_shape=(
            jax.ShapeDtypeStruct((UTTS, FRAMES, LABELS), F32),
            jax.ShapeDtypeStruct((UTTS, FRAMES, JOINT), F32),
            jax.ShapeDtypeStruct((UTTS, LABELS, JOINT), F32),
            jax.ShapeDtypeStruct((CHUNKS, VOCAB), F32),
        ),
        in_specs=[smem] * 3 + [vmem] * 3 + [anywhere] * 3,
        out_specs=(vmem,) * 4,
        scratch_shapes=scratch,
        compiler_params=pltpu.CompilerParams(
            collective_id=0, has_side_effects=True, vmem_limit_bytes=56 * 1024 * 1024
        ),
    )(
        frame_lengths, label_lengths, label_ids, enc_rows, pred_rows, out_weight, enc_weight, pred_weight,
        teacher.reshape(ROWS, LABELS, VOCAB),
    )


def solution(mesh):
    return jax.shard_map(
        per_device,
        mesh=mesh,
        in_specs=(
            P(None, "tm", None),
            P(None, "label", None),
            P(),
            P(),
            P(("tm", "label"), "vocab"),
            P(None, "tm", "label", "vocab"),
            P(None, "label"),
            P(),
            P(),
        ),
        out_specs=(
            P(None, "tm", "label"),
            P(None, "tm", None),
            P(None, "label", None),
            P(("tm", "label"), "vocab"),
        ),
        check_vma=False,
    )
```

time: 1140 us -> 107 us (0.09)
  waiting for transfers between devices: 842 us -> 0 us
  blocking collectives: 222 us -> 0 us
  Pallas kernels: 0 us -> 94.4 us
  matrix products: 17.4 us -> 0 us
  local copies, waits for them, and re-layouts: 26.7 us -> 11.8 us
  between operations: 14.6 us -> 0.64 us
  other arithmetic: 11.8 us -> 0 us
    all_gather x1 -> x0, waiting for transfers between devices: 574 us -> none  [per_device(): lax.all_gather(out_weight, ('tm', 'label'), axis=0, tiled=True)]
    unnamed x4 -> x0, waiting for transfers between devices: 241 us -> none
    psum x2 -> x0, blocking collectives: 222 us -> none  [the longest x1 133 us: per_device(): pred_sum = lax.psum(jnp.sum(slope, axis=1), ('tm', 'vocab'))]
    pallas_call x0 -> x1, Pallas kernels: none -> 94.4 us  [per_device(): pl.pallas_call(kernel, out_shape=(jax.ShapeDtypeStruct((UTTS, FRAMES, LAB...]
    psum x1 -> x0, waiting for transfers between devices: 26.9 us -> none  [per_device(): enc_sum = lax.psum(jnp.sum(slope, axis=2), ('label', 'vocab'))]
    dot_general x7 -> x0, matrix products: 17.4 us -> none  [the longest x1 6.94 us: per_device(): logits = jnp.dot(hidden, forward_weight, preferred_element_type=jnp.float32)]
    convert_element_type x3 -> x0, local copies, waits for them, and re-layouts: 12.3 us -> none  [the longest x2 11 us: per_device(): post = teacher.reshape(pairs, vocab_dev).astype(jnp.float32)]
  transfers between devices with their start and end apart: 3 -> 0, of which waited for: 3 -> 0; matrix products, arithmetic and copies ran while one was open for 3% -> 0% of each run, Pallas kernels for 0% -> 0%
where the time goes in v1:
time: 107 us
  Pallas kernels  94.4 us (88%)
  local copies, waits for them, and re-layouts  11.8 us (11%)
    pallas_call x1, Pallas kernels, per_device(): pl.pallas_call(kernel, out_shape=(jax.ShapeDtypeStruct((UTTS, FRAMES, LAB...  94.4 us
    unnamed x4, local copies, waits for them, and re-layouts  8.83 us
    pallas_call x2, local copies, waits for them, and re-layouts, per_device(): pl.pallas_call(kernel, out_shape=(jax.ShapeDtypeStruct((UTTS, FRAMES, LAB...  2.95 us

profile of v1, /device:TPU:1, one launch (start us, length us, event | category | flops | bytes accessed | tf_op | source)
XLA Modules:
  0.0 106.8 jit_solution(7883162367496681169)
XLA Ops:
  0.6 1.4 %copy.14.pred_rows = bf16[2,10,640]{2,1,0:T(8,128)(2,1)} copy(bf16[2,10,640]{2,0,1:T(2,128)(2,1)} %param.10) | data formatting | bytes 51200 | tf_op args[1]
  2.0 4.4 %copy.13 = bf16[2,24,10,2048]{3,2,1,0:T(8,128)(2,1)} copy(bf16[2,24,10,2048]{3,1,2,0:T(8,128)(2,1)} %param.14) | data formatting | bytes 3932160 | tf_op args[5]
  6.4 94.4 %shard_map.120 = (f32[2,24,10]{2,1,0:T(8,128)}, f32[2,24,640]{2,1,0:T(8,128)}, f32[2,10,640]{2,1,0:T(8,128)}, f32[5,2048]{1,0:T(8,128)}) custom-call(s32[2]{0:T(128)} %frame_len.1, s32[2]{0:T(128)} %label_len.1, s32[2,10]{1,0:T(2,128)} %ids.1, bf16[2,24,640]{2,1,0:T(8,128)(2,1)} %enc_rows.1, bf16[2,10,640]{2,1,0:T(8,128)(2,1)} %copy.14.pred_rows, ...), custom_call_target="tpu_custom_call" | custom-call | tf_op jit(solution)/shard_map/pallas_call | solution.py:453
  100.8 1.4 %copy.15 = f32[2,24,10]{1,0,2:T(2,128)} copy(f32[2,24,10]{2,1,0:T(8,128)} %get-tuple-element.4) | data formatting | bytes 3840 | tf_op jit(solution)/shard_map/pallas_call | solution.py:453
  102.3 1.5 %copy.16 = f32[2,10,640]{2,0,1:T(2,128)} copy(f32[2,10,640]{2,1,0:T(8,128)} %get-tuple-element.6) | data formatting | bytes 102400 | tf_op jit(solution)/shard_map/pallas_call | solution.py:453
  103.8 1.6 %copy.19 = f32[2,24,640]{2,1,0:T(8,128)} copy(f32[2,24,640]{2,1,0:T(8,128)} %get-tuple-element.13) | data formatting | bytes 245760
  105.4 1.5 %copy.20 = f32[5,2048]{1,0:T(8,128)} copy(f32[5,2048]{1,0:T(8,128)} %get-tuple-element.15) | data formatting | bytes 81920

commit v2 on v0

v2 whole, which is shorter than its diff:
```python
import functools

import jax
import jax.numpy as jnp
from jax import lax
from jax.experimental import pallas as pl
from jax.experimental.pallas import tpu as pltpu
from jax.sharding import PartitionSpec as P

MESH = pl.DeviceIdType.MESH
F32, BF16 = jnp.float32, jnp.bfloat16
label_weight = 0.5

SIZE = {"x": 4, "y": 4, "z": 8}
ORDERS = (("z", "y", "x"), ("z", "y", "x"), ("z", "x", "y"), ("z", "x", "y"), ("y", "x", "z"))
CHUNKS = len(ORDERS)
TRAVEL = (0, 2, 1, 3, 4)
SLOT = (0, 3, 1, 4, 2)
GATHER = (4, 0, 2, 1, 3)
PARTS = ((0, 2), (4,), (1, 3))
BLOCKS = 128
UTTS, FRAMES, LABELS = 2, 24, 10
ROWS = UTTS * FRAMES
PAIRS = ROWS * LABELS
PADDED = 512
JOINT = 640
VOCAB = 2048
TILES = VOCAB // 128
SIDE = 40
CODED = 7 * (256 + 16)
LEVELS = 32767.0


def distances(axis):
    n = SIZE[axis]
    return sorted(range(1, n), key=lambda d: -min(d, n - d))


def nt(a, b):
    return lax.dot_general(a, b, (((1,), (1,)), ((), ())), preferred_element_type=F32)


def nn(a, b):
    return jnp.dot(a, b, preferred_element_type=F32)


def split3(value):
    first = value.astype(BF16)
    rest = value - first.astype(F32)
    second = rest.astype(BF16)
    third = (rest - second.astype(F32)).astype(BF16)
    return first, second, third


def encode(block):
    rows = block.shape[0]
    tiles = block.reshape(rows // 16, 16, 128)
    peak = jnp.maximum(jnp.max(jnp.abs(tiles), axis=0), 1e-35)
    power = jnp.ceil(jnp.log2(peak) + 0.01)
    codes = jnp.round(tiles * (LEVELS * jnp.exp2(-power))[None]).reshape(rows, 128)
    return codes.astype(jnp.int32).astype(jnp.int16), power.astype(jnp.int32).astype(jnp.int16)


def decode(codes, power):
    rows = codes.shape[0]
    scale = jnp.exp2(power.astype(jnp.int32).astype(F32)) * (1.0 / LEVELS)
    tiles = codes.astype(jnp.int32).astype(F32).reshape(rows // 16, 16, 128)
    return (tiles * scale[None]).reshape(rows, 128)


def kernel(
    frame_len, label_len, ids, enc_rows, pred_rows, own_weight, enc_weight_hbm, pred_weight_hbm, teacher_hbm,
    loss_out, enc_out, pred_out, grad_out,
    raw, weight, wide, hidden, hidden_t, act, post, expo, dlog, teacher, enc_weight, pred_weight, perm,
    proj, stats, stats_in, term, coded, coded_in, mid_coded, mid_in, last_in,
    side, side_code, pair_in, y_in, x_in, zh_in, zl_in, side_nat, grads, grads_in, result,
    local_sem, send_sem, recv_sem,
):
    tm, lab, core = lax.axis_index("tm"), lax.axis_index("label"), lax.axis_index("vocab")
    at = {"x": tm // 4, "y": lab // 2, "z": (lab % 2) * 4 + tm % 4}

    def device(axis, coordinate):
        where = dict(at)
        where[axis] = coordinate
        return (where["x"] * 4 + where["z"] % 4, where["y"] * 2 + where["z"] // 4, core)

    def around(axis, distance):
        return lax.rem(at[axis] + distance, SIZE[axis])

    other_core = (tm, lab, 1 - core)
    sent = []

    def send(src, dst, target):
        number = len(sent)
        copy = pltpu.make_async_remote_copy(
            src_ref=src, dst_ref=dst, send_sem=send_sem.at[number], recv_sem=recv_sem.at[number],
            device_id=target, device_id_type=MESH,
        )
        copy.start()
        sent.append(copy)
        return copy

    def arrived(copies):
        for copy in copies:
            copy.wait_recv()

    barrier = pltpu.get_barrier_semaphore()
    partners = [device(a, around(a, d)) for a in "zyx" for d in distances(a)] + [other_core]
    for target in partners:
        pl.semaphore_signal(barrier, inc=1, device_id=target, device_id_type=MESH)

    local = []
    for number, (src, dst) in enumerate(((enc_weight_hbm, enc_weight), (pred_weight_hbm, pred_weight), (teacher_hbm, teacher))):
        copy = pltpu.make_async_copy(src, dst, local_sem.at[number])
        copy.start()
        local.append(copy)

    own = own_weight[...].astype(F32)
    for r in range(CHUNKS):
        for c in range(TILES):
            result[r, c : c + 1, :] = own[r : r + 1, c * 128 : (c + 1) * 128]

    def spot(r):
        first, middle, last = ORDERS[r]
        return (at[last] * SIZE[middle] + at[middle]) * SIZE[first] + at[first]

    for r in range(CHUNKS):
        raw[r, pl.ds(pl.multiple_of(spot(r) * 16, 16), 16), :] = result[r].astype(BF16)

    pl.semaphore_wait(barrier, len(partners))

    first_copies = {}
    for low, high in ((0, 2), (2, 4), (4, 5)):
        axis = ORDERS[low][0]
        block = raw.at[low:high, pl.ds(pl.multiple_of(spot(low) * 16, 16), 16), :]
        first_copies[low] = [send(block, block, device(axis, around(axis, d))) for d in distances(axis)]

    j = lax.broadcasted_iota(jnp.int32, (JOINT, BLOCKS), 0)
    block_at = lax.broadcasted_iota(jnp.int32, (JOINT, BLOCKS), 1)
    for r in range(CHUNKS):
        first, middle, last = ORDERS[r]
        n1, n2 = SIZE[first], SIZE[middle]
        coords = {first: block_at % n1, middle: (block_at // n1) % n2, last: block_at // (n1 * n2)}
        natural = coords["x"] * 32 + (coords["z"] % 4) * 8 + coords["y"] * 2 + coords["z"] // 4
        columns = slice(SLOT[r] * BLOCKS, (SLOT[r] + 1) * BLOCKS)
        perm[:, columns] = jnp.where(j == natural * CHUNKS + r, 1.0, 0.0).astype(BF16)

    second_copies = {}
    for r in GATHER:
        first, middle, last = ORDERS[r]
        if r in first_copies:
            arrived(first_copies[r])
        rows = SIZE[first] * 16
        block = raw.at[r, pl.ds(pl.multiple_of((at[last] * SIZE[middle] + at[middle]) * rows, 16), rows), :]
        second_copies[r] = [send(block, block, device(middle, around(middle, d))) for d in distances(middle)]

    local[0].wait()
    local[1].wait()
    proj[...] = jnp.zeros_like(proj)
    for b in range(UTTS):
        proj[b * FRAMES : (b + 1) * FRAMES, :] = enc_rows[b].astype(F32)
    for u in range(LABELS):
        proj[ROWS + UTTS * u : ROWS + UTTS * (u + 1), :] = pred_rows[u].astype(F32)
    proj[0:ROWS, :] = nn(proj[0:ROWS, :].astype(BF16), enc_weight[...])
    proj[ROWS : ROWS + 32, :] = nn(proj[ROWS : ROWS + 32, :].astype(BF16), pred_weight[...])
    proj[...] = sum(nn(part, perm[...]) for part in split3(proj[...]))

    def last_block(r, coordinate):
        first, middle, last = ORDERS[r]
        rows = SIZE[first] * SIZE[middle] * 16
        return pl.ds(pl.multiple_of(coordinate * rows, 16), rows)

    third_copies = {}
    for r in GATHER:
        last = ORDERS[r][2]
        arrived(second_copies[r])
        block = raw.at[r, last_block(r, at[last]), :]
        third_copies[r] = [send(block, block, device(last, around(last, d))) for d in distances(last)]

    for b in range(UTTS):
        for u in range(LABELS):
            start = (b * LABELS + u) * FRAMES
            row = ROWS + UTTS * u + b
            act[start : start + FRAMES, :] = jnp.tanh(proj[b * FRAMES : (b + 1) * FRAMES, :] + proj[row : row + 1, :])
    act[PAIRS:PADDED, :] = jnp.zeros((PADDED - PAIRS, JOINT), F32)
    hidden[...] = act[...].astype(BF16)
    hidden_t[...] = act[...].T.astype(BF16)

    local[2].wait()
    lanes = lax.broadcasted_iota(jnp.int32, (FRAMES, 128), 1)
    rows_at = lax.broadcasted_iota(jnp.int32, (FRAMES, 128), 0)

    def group(g):
        return pl.ds(pl.multiple_of(g * FRAMES, 8), FRAMES)

    def teacher_step(g, carry):
        total, ent = jnp.zeros((FRAMES, 128), F32), jnp.zeros((FRAMES, 128), F32)
        for c in range(TILES):
            part = teacher[g, :, c * 128 : (c + 1) * 128].astype(F32)
            post[group(g), c * 128 : (c + 1) * 128] = part
            total += part
            ent += part * jnp.log(part)
        total = jnp.sum(total, axis=1, keepdims=True)
        ent = jnp.sum(ent, axis=1, keepdims=True)
        stats[group(g), :] = jnp.where(lanes == 1, total, jnp.where(lanes == 2, ent, 0.0))
        return carry

    lax.fori_loop(0, UTTS * LABELS, teacher_step, 0)
    dlog[PAIRS:PADDED, :] = jnp.zeros((PADDED - PAIRS, VOCAB), BF16)

    def settle(r):
        arrived(third_copies[r])
        wide[...] = raw[r].astype(F32)
        base = SLOT[r] * BLOCKS
        for c in range(TILES):
            weight[base : base + BLOCKS, c * 128 : (c + 1) * 128] = wide[pl.ds(c, BLOCKS, stride=16), :].astype(BF16)

    done = 0
    for rows in PARTS:
        for r in rows:
            settle(r)
        depth = slice(done, done + len(rows) * BLOCKS)
        done += len(rows) * BLOCKS
        for start in range(0, VOCAB, 512):
            columns = slice(start, start + 512)
            product = nn(hidden[0:PAIRS, depth], weight[depth, columns])
            expo[:, columns] = product if depth.start == 0 else expo[:, columns] + product

    def local_id(g):
        utt = g // LABELS
        return ids[utt, g - LABELS * utt] - core * VOCAB

    def expo_step(g, carry):
        rows = group(g)
        emitted = local_id(g)
        zero = jnp.zeros((FRAMES, 128), F32)
        expsum, cross, picked = zero, zero, zero
        for c in range(TILES):
            columns = slice(c * 128, (c + 1) * 128)
            logits = expo[rows, columns]
            powers = jnp.exp(logits)
            expo[rows, columns] = powers
            expsum += powers
            cross += post[rows, columns] * logits
            picked += jnp.where(lanes == emitted - c * 128, logits, 0.0)
        expsum = jnp.sum(expsum, axis=1, keepdims=True)
        cross = jnp.sum(cross, axis=1, keepdims=True)
        picked = jnp.sum(picked, axis=1, keepdims=True)
        stats[rows, :] += jnp.where(lanes == 0, expsum, jnp.where(lanes == 3, cross, jnp.where(lanes == 4, picked, 0.0)))
        return carry

    lax.fori_loop(0, UTTS * LABELS, expo_step, 0, unroll=4)
    stats_copy = send(stats, stats_in, other_core)
    stats_copy.wait_recv()

    def valid(g):
        utt = g // LABELS
        frames, labels = jnp.where(utt == 1, frame_len[1], frame_len[0]), jnp.where(utt == 1, label_len[1], label_len[0])
        label_ok = jnp.where(lab * LABELS + g - LABELS * utt < labels, 1.0, 0.0)
        return jnp.where(tm * FRAMES + rows_at < frames, label_ok, 0.0)

    def dlog_step(pair, carry):
        scales = []
        for half in range(2):
            g = 2 * pair + half
            sums = stats[group(g), :] + stats_in[group(g), :]
            mask = valid(g)
            scales.append(
                (
                    (1.0 + label_weight) * mask / sums[:, 0:1],
                    mask / sums[:, 1:2],
                    label_weight * mask,
                    local_id(g),
                    group(g),
                )
            )
        for c in range(TILES):
            columns = slice(c * 128, (c + 1) * 128)
            parts = []
            for a, b, hot, emitted, rows in scales:
                value = a * expo[rows, columns] - b * post[rows, columns]
                parts.append(value - jnp.where(lanes == emitted - c * 128, hot, 0.0))
            dlog[pl.ds(pl.multiple_of(pair * 2 * FRAMES, 16), 2 * FRAMES), columns] = jnp.concatenate(parts, axis=0).astype(BF16)
        return carry

    lax.fori_loop(0, UTTS * LABELS // 2, dlog_step, 0, unroll=2)

    def ship(r, source, store, inbox, axis, rows, base):
        copies = []
        for d in distances(axis):
            start = base + around(axis, d) * rows
            codes, power = encode(source[r, pl.ds(pl.multiple_of(start, 16), rows), :])
            low = (d - 1) * (rows + 16)
            store[r, low : low + rows, :] = codes
            store[r, low + rows : low + rows + 16, :] = power
            place = slice(low, low + rows + 16)
            copies.append(send(store.at[r, place, :], inbox.at[r, place, :], device(axis, around(axis, d))))
        return copies

    def collect(r, copies, inbox, axis, rows, base):
        arrived(copies)
        place = pl.ds(pl.multiple_of(base + at[axis] * rows, 16), rows)
        total = term[r, place, :]
        for d in range(1, SIZE[axis]):
            low = (d - 1) * (rows + 16)
            total = total + decode(inbox[r, low : low + rows, :], inbox[r, low + rows : low + rows + 16, :])
        term[r, place, :] = total

    def sizes(r):
        first, middle, last = ORDERS[r]
        low = SIZE[first] * 16
        high = low * SIZE[middle]
        return low, high, at[last] * high, at[last] * high + at[middle] * low

    third = {}
    for r in TRAVEL:
        base = SLOT[r] * BLOCKS
        product = nn(hidden_t[base : base + BLOCKS, :], dlog[...])
        for c in range(TILES):
            term[r, pl.ds(c, BLOCKS, stride=16), :] = product[:, c * 128 : (c + 1) * 128]
        third[r] = ship(r, term, coded, coded_in, ORDERS[r][2], sizes(r)[1], 0)

    act[...] = nt(dlog[...], weight[...]) * (1.0 - act[...] * act[...])
    side[...] = jnp.zeros_like(side)
    for b in range(UTTS):
        over_labels = jnp.zeros((FRAMES, JOINT), F32)
        for u in range(LABELS):
            start = (b * LABELS + u) * FRAMES
            part = act[start : start + FRAMES, :]
            over_labels += part
            row = b * SIDE + FRAMES + u
            side[row : row + 1, :] = jnp.sum(part, axis=0, keepdims=True)
        side[b * SIDE : b * SIDE + FRAMES, :] = over_labels
    theirs = side.at[pl.ds(pl.multiple_of((1 - core) * SIDE, 8), SIDE), :]
    pair_copy = send(theirs, pair_in, other_core)

    second, first_hop = {}, {}

    def turn(r):
        low, high, start, _ = sizes(r)
        collect(r, third[r], coded_in, ORDERS[r][2], high, 0)
        second[r] = ship(r, term, mid_coded, mid_in, ORDERS[r][1], low, start)

    def finish(r):
        axis = ORDERS[r][0]
        size, _, start, place = sizes(r)
        collect(r, second[r], mid_in, ORDERS[r][1], size, start)
        first_hop[r] = []
        for d in distances(axis):
            block = term.at[r, pl.ds(pl.multiple_of(place + around(axis, d) * 16, 16), 16), :]
            first_hop[r].append(send(block, last_in.at[d - 1, r], device(axis, around(axis, d))))

    turn(TRAVEL[0])

    pair_copy.wait_recv()
    side_nat[...] = side[pl.ds(pl.multiple_of(core * SIDE, 8), SIDE), :] + pair_in[...]

    def fold(start, rows):
        strips = [side_nat[start : start + rows, k * 128 : (k + 1) * 128] for k in range(JOINT // 128)]
        if rows == FRAMES:
            strips.append(jnp.zeros((8, 128), F32))
        return jnp.concatenate(strips, axis=0)

    def code_side(slot):
        for start, rows, span, low in ((0, FRAMES, 128, 0), (FRAMES, SIDE - FRAMES, 80, 144)):
            codes, power = encode(fold(start, rows))
            side_code[slot, low : low + span, :] = codes
            side_code[slot, low + span : low + span + 16, :] = power

    def add_side(enc_ref, enc_count, pred_ref, pred_count):
        for ref, count, start, rows, span in ((enc_ref, enc_count, 0, FRAMES, 128), (pred_ref, pred_count, FRAMES, SIDE - FRAMES, 80)):
            total = decode(ref[0, 0:span, :], ref[0, span : span + 16, :])
            for d in range(1, count):
                total = total + decode(ref[d, 0:span, :], ref[d, span : span + 16, :])
            for k in range(JOINT // 128):
                side_nat[start : start + rows, k * 128 : (k + 1) * 128] += total[k * rows : (k + 1) * rows]

    code_side(0)
    enc_part, pred_part = side_code.at[0, 0:144, :], side_code.at[0, 144:240, :]
    y_copies = [send(enc_part, y_in.at[d - 1], device("y", around("y", d))) for d in distances("y")]
    x_copies = [send(pred_part, x_in.at[d - 1], device("x", around("x", d))) for d in distances("x")]

    turn(TRAVEL[1])

    for b in range(UTTS):
        for u in range(LABELS):
            g = b * LABELS + u
            rows = slice(g * FRAMES, (g + 1) * FRAMES)
            sums = stats[rows, :] + stats_in[rows, :]
            expsum, total, ent, cross, picked = (sums[:, k : k + 1] for k in range(5))
            lse = jnp.log(expsum)
            pair_loss = ent / total - jnp.log(total) - cross / total + lse + label_weight * (lse - picked)
            line = jnp.sum(jnp.where(lanes == rows_at, valid(g) * pair_loss, 0.0), axis=0, keepdims=True)
            loss_out[u, b : b + 1, :] = line[:, 0:FRAMES]

    turn(TRAVEL[2])
    turn(TRAVEL[3])
    finish(TRAVEL[0])
    finish(TRAVEL[1])

    arrived(y_copies + x_copies)
    add_side(y_in, 3, x_in, 3)
    code_side(1)
    z_low, z_high = at["z"] % 4, at["z"] // 4
    zh_copy = send(side_code.at[1, 0:144, :], zh_in.at[0], device("z", around("z", 4)))
    zl_copies = [
        send(side_code.at[1, 144:240, :], zl_in.at[d - 1], device("z", z_high * 4 + (z_low + d) % 4)) for d in range(1, 4)
    ]

    finish(TRAVEL[2])
    finish(TRAVEL[3])
    turn(TRAVEL[4])
    finish(TRAVEL[4])

    def stacked(value):
        return jnp.concatenate([part.astype(F32) for part in split3(value)], axis=0).astype(BF16)

    def unstacked(value):
        rows = value.shape[0] // 3
        return value[0:rows] + value[rows : 2 * rows] + value[2 * rows : 3 * rows]

    arrived([zh_copy] + zl_copies)
    add_side(zh_in, 1, zl_in, 3)
    natural = unstacked(nt(stacked(side_nat[...]), perm[...]))
    grads[0:FRAMES, :] = unstacked(nt(stacked(natural[0:FRAMES]), enc_weight[...]))
    grads[FRAMES:SIDE, :] = unstacked(nt(stacked(natural[FRAMES:SIDE]), pred_weight[...]))
    grads_copy = send(grads, grads_in, other_core)

    for r in TRAVEL:
        arrived(first_hop[r])
        total_r = term[r, pl.ds(pl.multiple_of(spot(r) * 16, 16), 16), :]
        for d in range(1, SIZE[ORDERS[r][0]]):
            total_r = total_r + last_in[d - 1, r]
        result[r] = total_r
        for c in range(TILES):
            grad_out[r : r + 1, c * 128 : (c + 1) * 128] = result[r, c : c + 1, :]

    grads_copy.wait_recv()
    enc_out[core] = grads[0:FRAMES, :]
    enc_out[1 - core] = grads_in[0:FRAMES, :]
    for u in range(LABELS):
        mine, other = grads[FRAMES + u : FRAMES + u + 1, :], grads_in[FRAMES + u : FRAMES + u + 1, :]
        pred_out[u, 0:1, :] = jnp.where(core == 0, mine, other)
        pred_out[u, 1:2, :] = jnp.where(core == 0, other, mine)

    for copy in sent:
        copy.wait_send()


def hand_over(*refs):
    half = len(refs) // 2
    for src, dst in zip(refs[:half], refs[half:]):
        dst[...] = src[...]


def per_device(
    enc_rows, pred_rows, enc_weight, pred_weight, out_weight, teacher, label_ids, frame_lengths, label_lengths
):
    vmem, smem, anywhere = (pl.BlockSpec(memory_space=s) for s in (pltpu.VMEM, pltpu.SMEM, pl.ANY))
    scratch = [
        pltpu.VMEM((CHUNKS, BLOCKS * 16, 128), BF16),
        pltpu.VMEM((JOINT, VOCAB), BF16),
        pltpu.VMEM((BLOCKS * 16, 128), F32),
        pltpu.VMEM((PADDED, JOINT), BF16),
        pltpu.VMEM((JOINT, PADDED), BF16),
        pltpu.VMEM((PADDED, JOINT), F32),
        pltpu.VMEM((PAIRS, VOCAB), F32),
        pltpu.VMEM((PAIRS, VOCAB), F32),
        pltpu.VMEM((PADDED, VOCAB), BF16),
        pltpu.VMEM((UTTS * LABELS, FRAMES, VOCAB), BF16),
        pltpu.VMEM((JOINT, JOINT), BF16),
        pltpu.VMEM((JOINT, JOINT), BF16),
        pltpu.VMEM((JOINT, JOINT), BF16),
        pltpu.VMEM((128, JOINT), F32),
        pltpu.VMEM((PAIRS, 128), F32),
        pltpu.VMEM((PAIRS, 128), F32),
        pltpu.VMEM((CHUNKS, BLOCKS * 16, 128), F32),
        pltpu.VMEM((CHUNKS, CODED, 128), jnp.int16),
        pltpu.VMEM((CHUNKS, CODED, 128), jnp.int16),
        pltpu.VMEM((CHUNKS, 3 * (128 + 16), 128), jnp.int16),
        pltpu.VMEM((CHUNKS, 3 * (128 + 16), 128), jnp.int16),
        pltpu.VMEM((7, CHUNKS, 16, 128), F32),
        pltpu.VMEM((2 * SIDE, JOINT), F32),
        pltpu.VMEM((2, 240, 128), jnp.int16),
        pltpu.VMEM((SIDE, JOINT), F32),
        pltpu.VMEM((3, 144, 128), jnp.int16),
        pltpu.VMEM((3, 96, 128), jnp.int16),
        pltpu.VMEM((1, 144, 128), jnp.int16),
        pltpu.VMEM((3, 96, 128), jnp.int16),
        pltpu.VMEM((SIDE, JOINT), F32),
        pltpu.VMEM((SIDE, JOINT), F32),
        pltpu.VMEM((SIDE, JOINT), F32),
        pltpu.VMEM((CHUNKS, 16, 128), F32),
        pltpu.SemaphoreType.DMA((3,)),
        pltpu.SemaphoreType.DMA((144,)),
        pltpu.SemaphoreType.DMA((144,)),
    ]
    shapes = (
        jax.ShapeDtypeStruct((LABELS, UTTS, FRAMES), F32),
        jax.ShapeDtypeStruct((UTTS, FRAMES, JOINT), F32),
        jax.ShapeDtypeStruct((LABELS, UTTS, JOINT), F32),
        jax.ShapeDtypeStruct((CHUNKS, VOCAB), F32),
    )
    results = pl.pallas_call(
        kernel,
        out_shape=shapes,
        in_specs=[smem] * 3 + [vmem] * 3 + [anywhere] * 3,
        out_specs=(vmem,) * 4,
        scratch_shapes=scratch,
        compiler_params=pltpu.CompilerParams(
            collective_id=0, has_side_effects=True, vmem_limit_bytes=56 * 1024 * 1024
        ),
    )(
        frame_lengths, label_lengths, label_ids, enc_rows, pred_rows.transpose(1, 0, 2), out_weight,
        enc_weight, pred_weight, teacher.transpose(0, 2, 1, 3).reshape(UTTS * LABELS, FRAMES, VOCAB),
    )
    loss, grad_enc, grad_pred, grad_out = pl.pallas_call(
        hand_over, out_shape=shapes, in_specs=[vmem] * 4, out_specs=(vmem,) * 4
    )(*results)
    return loss.transpose(1, 2, 0), grad_enc, grad_pred.transpose(1, 0, 2), grad_out


def solution(mesh):
    return jax.shard_map(
        per_device,
        mesh=mesh,
        in_specs=(
            P(None, "tm", None),
            P(None, "label", None),
            P(),
            P(),
            P(("tm", "label"), "vocab"),
            P(None, "tm", "label", "vocab"),
            P(None, "label"),
            P(),
            P(),
        ),
        out_specs=(
            P(None, "tm", "label"),
            P(None, "tm", None),
            P(None, "label", None),
            P(("tm", "label"), "vocab"),
        ),
        check_vma=False,
    )
```

time: 1140 us -> 73.7 us (0.06)
  waiting for transfers between devices: 842 us -> 0 us
  blocking collectives: 222 us -> 0 us
  Pallas kernels: 0 us -> 72.9 us
  local copies, waits for them, and re-layouts: 26.7 us -> 0 us
  matrix products: 17.4 us -> 0 us
  between operations: 14.6 us -> 0.64 us
  other arithmetic: 11.8 us -> 0 us
    all_gather x1 -> x0, waiting for transfers between devices: 574 us -> none  [per_device(): lax.all_gather(out_weight, ('tm', 'label'), axis=0, tiled=True)]
    unnamed x4 -> x0, waiting for transfers between devices: 241 us -> none
    psum x2 -> x0, blocking collectives: 222 us -> none  [the longest x1 133 us: per_device(): pred_sum = lax.psum(jnp.sum(slope, axis=1), ('tm', 'vocab'))]
    pallas_call x0 -> x2, Pallas kernels: none -> 72.9 us  [the longest x1 71.3 us: per_device(): pl.pallas_call(kernel, out_shape=shapes, in_specs=[smem] * 3 + [vmem] * 3...]
    psum x1 -> x0, waiting for transfers between devices: 26.9 us -> none  [per_device(): enc_sum = lax.psum(jnp.sum(slope, axis=2), ('label', 'vocab'))]
    dot_general x7 -> x0, matrix products: 17.4 us -> none  [the longest x1 6.94 us: per_device(): logits = jnp.dot(hidden, forward_weight, preferred_element_type=jnp.float32)]
    convert_element_type x3 -> x0, local copies, waits for them, and re-layouts: 12.3 us -> none  [the longest x2 11 us: per_device(): post = teacher.reshape(pairs, vocab_dev).astype(jnp.float32)]
  transfers between devices with their start and end apart: 3 -> 0, of which waited for: 3 -> 0; matrix products, arithmetic and copies ran while one was open for 3% -> 0% of each run, Pallas kernels for 0% -> 0%
where the time goes in v2:
time: 73.7 us; the launch traced here: 73.6 us
  Pallas kernels  72.9 us (99%)
    pallas_call x1, Pallas kernels, per_device(): pl.pallas_call(kernel, out_shape=shapes, in_specs=[smem] * 3 + [vmem] * 3...  71.3 us
    pallas_call x1, Pallas kernels, per_device(): pl.pallas_call(hand_over, out_shape=shapes, in_specs=[vmem] * 4, out_spec...  1.65 us

profile of v2, /device:TPU:1, one launch (start us, length us, event | category | flops | bytes accessed | tf_op | source)
XLA Modules:
  0.0 73.6 jit_solution(18269287201591455399)
XLA Ops:
  0.6 71.3 %shard_map.120 = (f32[10,2,24]{2,1,0:T(2,128)}, f32[2,24,640]{2,1,0:T(8,128)}, f32[10,2,640]{2,1,0:T(2,128)}, f32[5,2048]{1,0:T(8,128)}) custom-call(s32[2]{0:T(128)} %frame_len.1, s32[2]{0:T(128)} %label_len.1, s32[2,10]{1,0:T(2,128)} %ids.1, bf16[2,24,640]{2,1,0:T(8,128)(2,1)} %enc_rows.1, bf16[10,2,640]{2,1,0:T(2,128)(2,1)} %bitcast.7, ...), custom_call_target="tpu_custom_call" | custom-call | tf_op jit(solution)/shard_map/pallas_call | solution.py:504
  71.9 1.6 %shard_map.121 = (f32[10,2,24]{2,1,0:T(2,128)}, f32[2,24,640]{2,1,0:T(8,128)}, f32[10,2,640]{2,1,0:T(2,128)}, f32[5,2048]{1,0:T(8,128)}) custom-call(f32[10,2,24]{2,1,0:T(2,128)} %get-tuple-element.12.refs_0_, f32[2,24,640]{2,1,0:T(8,128)} %get-tuple-element.13.refs_1_, f32[10,2,640]{2,1,0:T(2,128)} %get-tuple-element.14.refs_2_, ...), custom_call_target="tpu_custom_call" | custom-call | tf_op jit(solution)/shard_map/pallas_call | solution.py:517

commit v3 on v2

--- a/solution.py
+++ b/solution.py
@@ -14,7 +14,7 @@
 SIZE = {"x": 4, "y": 4, "z": 8}
 ORDERS = (("z", "y", "x"), ("z", "y", "x"), ("z", "x", "y"), ("z", "x", "y"), ("y", "x", "z"))
 CHUNKS = len(ORDERS)
-TRAVEL = (0, 2, 1, 3, 4)
+TRAVEL = (4, 0, 2, 1, 3)
 SLOT = (0, 3, 1, 4, 2)
 GATHER = (4, 0, 2, 1, 3)
 PARTS = ((0, 2), (4,), (1, 3))
@@ -69,10 +69,10 @@
 
 
 def kernel(
-    frame_len, label_len, ids, enc_rows, pred_rows, own_weight, enc_weight_hbm, pred_weight_hbm, teacher_hbm,
+    frame_len, label_len, ids, enc_rows_hbm, pred_rows_hbm, own_weight_hbm, enc_weight_hbm, pred_weight_hbm, teacher_hbm,
     loss_out, enc_out, pred_out, grad_out,
-    raw, weight, wide, hidden, hidden_t, act, post, expo, dlog, teacher, enc_weight, pred_weight, perm,
-    proj, stats, stats_in, term, coded, coded_in, mid_coded, mid_in, last_in,
+    enc_rows, pred_rows, own_weight, raw, weight, wide, hidden, hidden_t, act, post, expo, dlog, teacher, enc_weight, pred_weight, perm,
+    proj, stats, stats_in, term, coded, coded_in, mid_coded, mid_in, last_code, last_in,
     side, side_code, pair_in, y_in, x_in, zh_in, zl_in, side_nat, grads, grads_in, result,
     local_sem, send_sem, recv_sem,
 ):
@@ -100,6 +100,13 @@
         sent.append(copy)
         return copy
 
+    left = [0]
+
+    def drain():
+        for copy in sent[left[0] :]:
+            copy.wait_send()
+        left[0] = len(sent)
+
     def arrived(copies):
         for copy in copies:
             copy.wait_recv()
@@ -110,11 +117,16 @@
         pl.semaphore_signal(barrier, inc=1, device_id=target, device_id_type=MESH)
 
     local = []
-    for number, (src, dst) in enumerate(((enc_weight_hbm, enc_weight), (pred_weight_hbm, pred_weight), (teacher_hbm, teacher))):
+    moves = (
+        (own_weight_hbm, own_weight), (enc_rows_hbm, enc_rows), (pred_rows_hbm, pred_rows),
+        (enc_weight_hbm, enc_weight), (pred_weight_hbm, pred_weight), (teacher_hbm, teacher),
+    )
+    for number, (src, dst) in enumerate(moves):
         copy = pltpu.make_async_copy(src, dst, local_sem.at[number])
         copy.start()
         local.append(copy)
 
+    local[0].wait()
     own = own_weight[...].astype(F32)
     for r in range(CHUNKS):
         for c in range(TILES):
@@ -154,8 +166,8 @@
         block = raw.at[r, pl.ds(pl.multiple_of((at[last] * SIZE[middle] + at[middle]) * rows, 16), rows), :]
         second_copies[r] = [send(block, block, device(middle, around(middle, d))) for d in distances(middle)]
 
-    local[0].wait()
-    local[1].wait()
+    for copy in local[1:5]:
+        copy.wait()
     proj[...] = jnp.zeros_like(proj)
     for b in range(UTTS):
         proj[b * FRAMES : (b + 1) * FRAMES, :] = enc_rows[b].astype(F32)
@@ -170,12 +182,36 @@
         rows = SIZE[first] * SIZE[middle] * 16
         return pl.ds(pl.multiple_of(coordinate * rows, 16), rows)
 
+    def part_block(r, coordinate, half):
+        first, middle, last = ORDERS[r]
+        rows = SIZE[first] * SIZE[middle] * 16
+        return pl.ds(pl.multiple_of(coordinate * rows + half * (rows // 2), 16), rows // 2)
+
     third_copies = {}
     for r in GATHER:
         last = ORDERS[r][2]
         arrived(second_copies[r])
         block = raw.at[r, last_block(r, at[last]), :]
-        third_copies[r] = [send(block, block, device(last, around(last, d))) for d in distances(last)]
+        third_copies[r] = {
+            d: send(block, block, device(last, around(last, SIZE[last] + d))) for d in ((2, -2, 1, -1) if SIZE[last] == 8 else (1, -1))
+        }
+
+    def hand_on(r):
+        last = ORDERS[r][2]
+        n = SIZE[last]
+        near = n // 4
+        copies = third_copies[r]
+        more = []
+        for way, half in ((1, 0), (-1, 1)):
+            copies[way * near].wait_recv()
+            source = around(last, n - way * near)
+            place = part_block(r, source, half)
+            block = raw.at[r, place, :]
+            more.append(send(block, block, device(last, around(last, n + way * near))))
+            if n == 8:
+                block = raw.at[r, last_block(r, source), :]
+                more.append(send(block, block, device(last, around(last, n + way))))
+        third_copies[r] = more + ([copies[1], copies[-1]] if n == 8 else [])
 
     for b in range(UTTS):
         for u in range(LABELS):
@@ -186,7 +222,7 @@
     hidden[...] = act[...].astype(BF16)
     hidden_t[...] = act[...].T.astype(BF16)
 
-    local[2].wait()
+    local[5].wait()
     lanes = lax.broadcasted_iota(jnp.int32, (FRAMES, 128), 1)
     rows_at = lax.broadcasted_iota(jnp.int32, (FRAMES, 128), 0)
 
@@ -205,8 +241,13 @@
         stats[group(g), :] = jnp.where(lanes == 1, total, jnp.where(lanes == 2, ent, 0.0))
         return carry
 
-    lax.fori_loop(0, UTTS * LABELS, teacher_step, 0)
+    lax.fori_loop(0, 10, teacher_step, 0)
+    for r in GATHER[:3]:
+        hand_on(r)
+    lax.fori_loop(10, UTTS * LABELS, teacher_step, 0)
     dlog[PAIRS:PADDED, :] = jnp.zeros((PADDED - PAIRS, VOCAB), BF16)
+    for r in GATHER[3:]:
+        hand_on(r)
 
     def settle(r):
         arrived(third_copies[r])
@@ -312,13 +353,21 @@
         high = low * SIZE[middle]
         return low, high, at[last] * high, at[last] * high + at[middle] * low
 
+    gathered = len(sent)
     third = {}
-    for r in TRAVEL:
+
+    def multiply(r):
         base = SLOT[r] * BLOCKS
         product = nn(hidden_t[base : base + BLOCKS, :], dlog[...])
         for c in range(TILES):
             term[r, pl.ds(c, BLOCKS, stride=16), :] = product[:, c * 128 : (c + 1) * 128]
+
+    def depart(r):
         third[r] = ship(r, term, coded, coded_in, ORDERS[r][2], sizes(r)[1], 0)
+
+    for r in (4, 0, 2):
+        multiply(r)
+        depart(r)
 
     act[...] = nt(dlog[...], weight[...]) * (1.0 - act[...] * act[...])
     side[...] = jnp.zeros_like(side)
@@ -341,17 +390,26 @@
         collect(r, third[r], coded_in, ORDERS[r][2], high, 0)
         second[r] = ship(r, term, mid_coded, mid_in, ORDERS[r][1], low, start)
 
-    def finish(r):
-        axis = ORDERS[r][0]
-        size, _, start, place = sizes(r)
-        collect(r, second[r], mid_in, ORDERS[r][1], size, start)
-        first_hop[r] = []
+    def finish(low, high):
+        axis = ORDERS[low][0]
+        size, _, start, place = sizes(low)
+        for r in range(low, high):
+            collect(r, second[r], mid_in, ORDERS[r][1], size, start)
+        first_hop[low] = []
+        rows, base = (high - low) * 16, low * 24
         for d in distances(axis):
-            block = term.at[r, pl.ds(pl.multiple_of(place + around(axis, d) * 16, 16), 16), :]
-            first_hop[r].append(send(block, last_in.at[d - 1, r], device(axis, around(axis, d))))
-
-    turn(TRAVEL[0])
-
+            spot_d = pl.ds(pl.multiple_of(place + around(axis, d) * 16, 16), 16)
+            codes, power = encode(jnp.concatenate([term[r, spot_d, :] for r in range(low, high)], axis=0))
+            last_code[d - 1, base : base + rows, :] = codes
+            last_code[d - 1, base + rows : base + rows + 16, :] = power
+            block = slice(base, base + rows + 16)
+            first_hop[low].append(send(last_code.at[d - 1, block, :], last_in.at[d - 1, block, :], device(axis, around(axis, d))))
+
+    for copy in sent[:gathered]:
+        copy.wait_send()
+    left[0] = gathered
+
+    multiply(1)
     pair_copy.wait_recv()
     side_nat[...] = side[pl.ds(pl.multiple_of(core * SIDE, 8), SIDE), :] + pair_in[...]
 
@@ -380,7 +438,9 @@
     y_copies = [send(enc_part, y_in.at[d - 1], device("y", around("y", d))) for d in distances("y")]
     x_copies = [send(pred_part, x_in.at[d - 1], device("x", around("x", d))) for d in distances("x")]
 
-    turn(TRAVEL[1])
+    depart(1)
+    multiply(3)
+    depart(3)
 
     for b in range(UTTS):
         for u in range(LABELS):
@@ -393,10 +453,8 @@
             line = jnp.sum(jnp.where(lanes == rows_at, valid(g) * pair_loss, 0.0), axis=0, keepdims=True)
             loss_out[u, b : b + 1, :] = line[:, 0:FRAMES]
 
-    turn(TRAVEL[2])
-    turn(TRAVEL[3])
-    finish(TRAVEL[0])
-    finish(TRAVEL[1])
+    turn(0)
+    turn(2)
 
     arrived(y_copies + x_copies)
     add_side(y_in, 3, x_in, 3)
@@ -407,10 +465,14 @@
         send(side_code.at[1, 144:240, :], zl_in.at[d - 1], device("z", z_high * 4 + (z_low + d) % 4)) for d in range(1, 4)
     ]
 
-    finish(TRAVEL[2])
-    finish(TRAVEL[3])
-    turn(TRAVEL[4])
-    finish(TRAVEL[4])
+    turn(4)
+    turn(1)
+    turn(3)
+    drain()
+    finish(4, 5)
+
+    finish(0, 2)
+    finish(2, 4)
 
     def stacked(value):
         return jnp.concatenate([part.astype(F32) for part in split3(value)], axis=0).astype(BF16)
@@ -426,14 +488,19 @@
     grads[FRAMES:SIDE, :] = unstacked(nt(stacked(natural[FRAMES:SIDE]), pred_weight[...]))
     grads_copy = send(grads, grads_in, other_core)
 
-    for r in TRAVEL:
-        arrived(first_hop[r])
-        total_r = term[r, pl.ds(pl.multiple_of(spot(r) * 16, 16), 16), :]
-        for d in range(1, SIZE[ORDERS[r][0]]):
-            total_r = total_r + last_in[d - 1, r]
-        result[r] = total_r
-        for c in range(TILES):
-            grad_out[r : r + 1, c * 128 : (c + 1) * 128] = result[r, c : c + 1, :]
+    drain()
+    for low, high in ((4, 5), (0, 2), (2, 4)):
+        arrived(first_hop[low])
+        rows, base = (high - low) * 16, low * 24
+        total = jnp.concatenate(
+            [term[r, pl.ds(pl.multiple_of(spot(r) * 16, 16), 16), :] for r in range(low, high)], axis=0
+        )
+        for d in distances(ORDERS[low][0]):
+            total = total + decode(last_in[d - 1, base : base + rows, :], last_in[d - 1, base + rows : base + rows + 16, :])
+        for r in range(low, high):
+            result[r] = total[(r - low) * 16 : (r - low + 1) * 16]
+            for c in range(TILES):
+                grad_out[r : r + 1, c * 128 : (c + 1) * 128] = result[r, c : c + 1, :]
 
     grads_copy.wait_recv()
     enc_out[core] = grads[0:FRAMES, :]
@@ -443,8 +510,7 @@
         pred_out[u, 0:1, :] = jnp.where(core == 0, mine, other)
         pred_out[u, 1:2, :] = jnp.where(core == 0, other, mine)
 
-    for copy in sent:
-        copy.wait_send()
+    drain()
 
 
 def hand_over(*refs):
@@ -458,6 +524,9 @@
 ):
     vmem, smem, anywhere = (pl.BlockSpec(memory_space=s) for s in (pltpu.VMEM, pltpu.SMEM, pl.ANY))
     scratch = [
+        pltpu.VMEM((UTTS, FRAMES, JOINT), BF16),
+        pltpu.VMEM((LABELS, UTTS, JOINT), BF16),
+        pltpu.VMEM((CHUNKS, VOCAB), BF16),
         pltpu.VMEM((CHUNKS, BLOCKS * 16, 128), BF16),
         pltpu.VMEM((JOINT, VOCAB), BF16),
         pltpu.VMEM((BLOCKS * 16, 128), F32),
@@ -479,7 +548,8 @@
         pltpu.VMEM((CHUNKS, CODED, 128), jnp.int16),
         pltpu.VMEM((CHUNKS, 3 * (128 + 16), 128), jnp.int16),
         pltpu.VMEM((CHUNKS, 3 * (128 + 16), 128), jnp.int16),
-        pltpu.VMEM((7, CHUNKS, 16, 128), F32),
+        pltpu.VMEM((7, 128, 128), jnp.int16),
+        pltpu.VMEM((7, 128, 128), jnp.int16),
         pltpu.VMEM((2 * SIDE, JOINT), F32),
         pltpu.VMEM((2, 240, 128), jnp.int16),
         pltpu.VMEM((SIDE, JOINT), F32),
@@ -491,7 +561,7 @@
         pltpu.VMEM((SIDE, JOINT), F32),
         pltpu.VMEM((SIDE, JOINT), F32),
         pltpu.VMEM((CHUNKS, 16, 128), F32),
-        pltpu.SemaphoreType.DMA((3,)),
+        pltpu.SemaphoreType.DMA((6,)),
         pltpu.SemaphoreType.DMA((144,)),
         pltpu.SemaphoreType.DMA((144,)),
     ]
@@ -504,7 +574,7 @@
     results = pl.pallas_call(
         kernel,
         out_shape=shapes,
-        in_specs=[smem] * 3 + [vmem] * 3 + [anywhere] * 3,
+        in_specs=[smem] * 3 + [anywhere] * 6,
         out_specs=(vmem,) * 4,
         scratch_shapes=scratch,
         compiler_params=pltpu.CompilerParams(

time: 73.7 us -> 70.3 us (0.954)
  Pallas kernels: 72.9 us -> 69.6 us
    pallas_call x1, Pallas kernels: 71.3 us -> 67.9 us  [per_device(): pl.pallas_call(kernel, out_shape=shapes, in_specs=[smem] * 3 + [anywhere]...]
where the time goes in v3:
time: 70.3 us; the launch traced here: 70.2 us
  Pallas kernels  69.6 us (99%)
    pallas_call x1, Pallas kernels, per_device(): pl.pallas_call(kernel, out_shape=shapes, in_specs=[smem] * 3 + [anywhere]...  67.9 us
    pallas_call x1, Pallas kernels, per_device(): pl.pallas_call(hand_over, out_shape=shapes, in_specs=[vmem] * 4, out_spec...  1.65 us

profile of v3, /device:TPU:1, one launch (start us, length us, event | category | flops | bytes accessed | tf_op | source)
XLA Modules:
  0.0 70.2 jit_solution(3341168253441673773)
XLA Ops:
  0.6 67.9 %shard_map.120 = (f32[10,2,24]{2,1,0:T(2,128)}, f32[2,24,640]{2,1,0:T(8,128)}, f32[10,2,640]{2,1,0:T(2,128)}, f32[5,2048]{1,0:T(8,128)}) custom-call(s32[2]{0:T(128)} %frame_len.1, s32[2]{0:T(128)} %label_len.1, s32[2,10]{1,0:T(2,128)} %ids.1, bf16[2,24,640]{2,1,0:T(8,128)(2,1)} %enc_rows_hbm.1, bf16[10,2,640]{2,1,0:T(2,128)(2,1)} %bitcast.7, ...), custom_call_target="tpu_custom_call" | custom-call | tf_op jit(solution)/shard_map/pallas_call | solution.py:574
  68.6 1.6 %shard_map.121 = (f32[10,2,24]{2,1,0:T(2,128)}, f32[2,24,640]{2,1,0:T(8,128)}, f32[10,2,640]{2,1,0:T(2,128)}, f32[5,2048]{1,0:T(8,128)}) custom-call(f32[10,2,24]{2,1,0:T(2,128)} %get-tuple-element.12.refs_0_, f32[2,24,640]{2,1,0:T(8,128)} %get-tuple-element.13.refs_1_, f32[10,2,640]{2,1,0:T(2,128)} %get-tuple-element.14.refs_2_, ...), custom_call_target="tpu_custom_call" | custom-call | tf_op jit(solution)/shard_map/pallas_call | solution.py:587

commit v4 on v3

--- a/solution.py
+++ b/solution.py
@@ -69,9 +69,9 @@
 
 
 def kernel(
-    frame_len, label_len, ids, enc_rows_hbm, pred_rows_hbm, own_weight_hbm, enc_weight_hbm, pred_weight_hbm, teacher_hbm,
+    frame_len_hbm, label_len_hbm, ids_hbm, enc_rows_hbm, pred_rows_hbm, own_weight_hbm, enc_weight_hbm, pred_weight_hbm, teacher_hbm,
     loss_out, enc_out, pred_out, grad_out,
-    enc_rows, pred_rows, own_weight, raw, weight, wide, hidden, hidden_t, act, post, expo, dlog, teacher, enc_weight, pred_weight, perm,
+    frame_len, label_len, ids, enc_rows, pred_rows, own_weight, raw, weight, wide, hidden, hidden_t, act, post, expo, dlog, teacher, enc_weight, pred_weight, perm,
     proj, stats, stats_in, term, coded, coded_in, mid_coded, mid_in, last_code, last_in,
     side, side_code, pair_in, y_in, x_in, zh_in, zl_in, side_nat, grads, grads_in, result,
     local_sem, send_sem, recv_sem,
@@ -120,6 +120,7 @@
     moves = (
         (own_weight_hbm, own_weight), (enc_rows_hbm, enc_rows), (pred_rows_hbm, pred_rows),
         (enc_weight_hbm, enc_weight), (pred_weight_hbm, pred_weight), (teacher_hbm, teacher),
+        (frame_len_hbm, frame_len), (label_len_hbm, label_len), (ids_hbm, ids),
     )
     for number, (src, dst) in enumerate(moves):
         copy = pltpu.make_async_copy(src, dst, local_sem.at[number])
@@ -222,7 +223,8 @@
     hidden[...] = act[...].astype(BF16)
     hidden_t[...] = act[...].T.astype(BF16)
 
-    local[5].wait()
+    for copy in local[5:]:
+        copy.wait()
     lanes = lax.broadcasted_iota(jnp.int32, (FRAMES, 128), 1)
     rows_at = lax.broadcasted_iota(jnp.int32, (FRAMES, 128), 0)
 
@@ -290,7 +292,7 @@
         stats[rows, :] += jnp.where(lanes == 0, expsum, jnp.where(lanes == 3, cross, jnp.where(lanes == 4, picked, 0.0)))
         return carry
 
-    lax.fori_loop(0, UTTS * LABELS, expo_step, 0, unroll=4)
+    lax.fori_loop(0, UTTS * LABELS, expo_step, 0, unroll=10)
     stats_copy = send(stats, stats_in, other_core)
     stats_copy.wait_recv()
 
@@ -324,7 +326,7 @@
             dlog[pl.ds(pl.multiple_of(pair * 2 * FRAMES, 16), 2 * FRAMES), columns] = jnp.concatenate(parts, axis=0).astype(BF16)
         return carry
 
-    lax.fori_loop(0, UTTS * LABELS // 2, dlog_step, 0, unroll=2)
+    lax.fori_loop(0, UTTS * LABELS // 2, dlog_step, 0, unroll=5)
 
     def ship(r, source, store, inbox, axis, rows, base):
         copies = []
@@ -468,7 +470,6 @@
     turn(4)
     turn(1)
     turn(3)
-    drain()
     finish(4, 5)
 
     finish(0, 2)
@@ -488,7 +489,6 @@
     grads[FRAMES:SIDE, :] = unstacked(nt(stacked(natural[FRAMES:SIDE]), pred_weight[...]))
     grads_copy = send(grads, grads_in, other_core)
 
-    drain()
     for low, high in ((4, 5), (0, 2), (2, 4)):
         arrived(first_hop[low])
         rows, base = (high - low) * 16, low * 24
@@ -522,8 +522,11 @@
 def per_device(
     enc_rows, pred_rows, enc_weight, pred_weight, out_weight, teacher, label_ids, frame_lengths, label_lengths
 ):
-    vmem, smem, anywhere = (pl.BlockSpec(memory_space=s) for s in (pltpu.VMEM, pltpu.SMEM, pl.ANY))
+    vmem, anywhere = (pl.BlockSpec(memory_space=s) for s in (pltpu.VMEM, pl.ANY))
     scratch = [
+        pltpu.SMEM((UTTS,), jnp.int32),
+        pltpu.SMEM((UTTS,), jnp.int32),
+        pltpu.SMEM((UTTS, LABELS), jnp.int32),
         pltpu.VMEM((UTTS, FRAMES, JOINT), BF16),
         pltpu.VMEM((LABELS, UTTS, JOINT), BF16),
         pltpu.VMEM((CHUNKS, VOCAB), BF16),
@@ -561,7 +564,7 @@
         pltpu.VMEM((SIDE, JOINT), F32),
         pltpu.VMEM((SIDE, JOINT), F32),
         pltpu.VMEM((CHUNKS, 16, 128), F32),
-        pltpu.SemaphoreType.DMA((6,)),
+        pltpu.SemaphoreType.DMA((9,)),
         pltpu.SemaphoreType.DMA((144,)),
         pltpu.SemaphoreType.DMA((144,)),
     ]
@@ -574,7 +577,7 @@
     results = pl.pallas_call(
         kernel,
         out_shape=shapes,
-        in_specs=[smem] * 3 + [anywhere] * 6,
+        in_specs=[anywhere] * 9,
         out_specs=(vmem,) * 4,
         scratch_shapes=scratch,
         compiler_params=pltpu.CompilerParams(

time: 70.3 us -> 69.7 us (level)
  no operation moved by 1% of the time
where the time goes in v4:
time: 69.7 us; the launch traced here: 69.6 us
  Pallas kernels  68.9 us (99%)
    pallas_call x1, Pallas kernels, per_device(): pl.pallas_call(kernel, out_shape=shapes, in_specs=[anywhere] * 9, out_spe...  67.3 us
    pallas_call x1, Pallas kernels, per_device(): pl.pallas_call(hand_over, out_shape=shapes, in_specs=[vmem] * 4, out_spec...  1.65 us

profile of v4, /device:TPU:1, one launch (start us, length us, event | category | flops | bytes accessed | tf_op | source)
XLA Modules:
  0.0 69.6 jit_solution(15980835470311880817)
XLA Ops:
  0.6 67.3 %shard_map.120 = (f32[10,2,24]{2,1,0:T(2,128)}, f32[2,24,640]{2,1,0:T(8,128)}, f32[10,2,640]{2,1,0:T(2,128)}, f32[5,2048]{1,0:T(8,128)}) custom-call(s32[2]{0:T(128)} %frame_len_hbm.1, s32[2]{0:T(128)} %label_len_hbm.1, s32[2,10]{1,0:T(2,128)} %ids_hbm.1, bf16[2,24,640]{2,1,0:T(8,128)(2,1)} %enc_rows_hbm.1, bf16[10,2,640]{2,1,0:T(2,128)(2,1)} %bitcast.7, ...), custom_call_target="tpu_custom_call" | custom-call | tf_op jit(solution)/shard_map/pallas_call | solution.py:577
  67.9 1.6 %shard_map.121 = (f32[10,2,24]{2,1,0:T(2,128)}, f32[2,24,640]{2,1,0:T(8,128)}, f32[10,2,640]{2,1,0:T(2,128)}, f32[5,2048]{1,0:T(8,128)}) custom-call(f32[10,2,24]{2,1,0:T(2,128)} %get-tuple-element.12.refs_0_, f32[2,24,640]{2,1,0:T(8,128)} %get-tuple-element.13.refs_1_, f32[10,2,640]{2,1,0:T(2,128)} %get-tuple-element.14.refs_2_, ...), custom_call_target="tpu_custom_call" | custom-call | tf_op jit(solution)/shard_map/pallas_call | solution.py:590

commit v5 on v4

--- a/solution.py
+++ b/solution.py
@@ -292,9 +292,11 @@
         stats[rows, :] += jnp.where(lanes == 0, expsum, jnp.where(lanes == 3, cross, jnp.where(lanes == 4, picked, 0.0)))
         return carry
 
-    lax.fori_loop(0, UTTS * LABELS, expo_step, 0, unroll=10)
-    stats_copy = send(stats, stats_in, other_core)
-    stats_copy.wait_recv()
+    stats_copies = []
+    for b in range(UTTS):
+        lax.fori_loop(b * LABELS, (b + 1) * LABELS, expo_step, 0, unroll=10)
+        rows = slice(b * LABELS * FRAMES, (b + 1) * LABELS * FRAMES)
+        stats_copies.append(send(stats.at[rows, :], stats_in.at[rows, :], other_core))
 
     def valid(g):
         utt = g // LABELS
@@ -326,7 +328,9 @@
             dlog[pl.ds(pl.multiple_of(pair * 2 * FRAMES, 16), 2 * FRAMES), columns] = jnp.concatenate(parts, axis=0).astype(BF16)
         return carry
 
-    lax.fori_loop(0, UTTS * LABELS // 2, dlog_step, 0, unroll=5)
+    for b in range(UTTS):
+        stats_copies[b].wait_recv()
+        lax.fori_loop(b * LABELS // 2, (b + 1) * LABELS // 2, dlog_step, 0, unroll=5)
 
     def ship(r, source, store, inbox, axis, rows, base):
         copies = []

time: 69.7 us -> 69 us (0.990)
  no operation moved by 1% of the time
where the time goes in v5:
time: 69 us; the launch traced here: 68.9 us
  Pallas kernels  68.3 us (99%)
    pallas_call x1, Pallas kernels, per_device(): pl.pallas_call(kernel, out_shape=shapes, in_specs=[anywhere] * 9, out_spe...  66.6 us
    pallas_call x1, Pallas kernels, per_device(): pl.pallas_call(hand_over, out_shape=shapes, in_specs=[vmem] * 4, out_spec...  1.65 us

profile of v5, /device:TPU:1, one launch (start us, length us, event | category | flops | bytes accessed | tf_op | source)
XLA Modules:
  0.0 68.9 jit_solution(8677426054767714913)
XLA Ops:
  0.6 66.6 %shard_map.120 = (f32[10,2,24]{2,1,0:T(2,128)}, f32[2,24,640]{2,1,0:T(8,128)}, f32[10,2,640]{2,1,0:T(2,128)}, f32[5,2048]{1,0:T(8,128)}) custom-call(s32[2]{0:T(128)} %frame_len_hbm.1, s32[2]{0:T(128)} %label_len_hbm.1, s32[2,10]{1,0:T(2,128)} %ids_hbm.1, bf16[2,24,640]{2,1,0:T(8,128)(2,1)} %enc_rows_hbm.1, bf16[10,2,640]{2,1,0:T(2,128)(2,1)} %bitcast.7, ...), custom_call_target="tpu_custom_call" | custom-call | tf_op jit(solution)/shard_map/pallas_call | solution.py:581
  67.3 1.6 %shard_map.121 = (f32[10,2,24]{2,1,0:T(2,128)}, f32[2,24,640]{2,1,0:T(8,128)}, f32[10,2,640]{2,1,0:T(2,128)}, f32[5,2048]{1,0:T(8,128)}) custom-call(f32[10,2,24]{2,1,0:T(2,128)} %get-tuple-element.12.refs_0_, f32[2,24,640]{2,1,0:T(8,128)} %get-tuple-element.13.refs_1_, f32[10,2,640]{2,1,0:T(2,128)} %get-tuple-element.14.refs_2_, ...), custom_call_target="tpu_custom_call" | custom-call | tf_op jit(solution)/shard_map/pallas_call | solution.py:594
